TPU v7x, 32 devices: a whole 2x2x4 slice. The times are simulated.
32 devices in a mesh: traj: 4 (over y, x), slab: 8 (over z, core).
Axes of the slice: x: 2, y: 2, z: 4, core: 2. Of those that a mesh axis runs over, the one named last changes fastest.
Arguments:
- grad_out: bfloat16 [64, 24, 128], P(('traj', 'slab')), parts along dimension 0, may hold values from -24 to 24
- cached: bfloat16 [64, 24, 128], P('traj', 'slab'), parts along dimension 0, may hold values from -0.059814453 to 0.059814453
- values: bfloat16 [64, 24, 128], P(('traj', 'slab')), parts along dimension 0, may hold values from -0.1796875 to 0.1796875
- query_x: bfloat16 [64, 128], P('traj'), parts along dimension 0, may hold values from -6 to 6
- key_x: bfloat16 [64, 128], P('traj'), parts along dimension 0, may hold values from -6 to 6
- query_y: bfloat16 [96, 128], P('traj'), parts along dimension 0, may hold values from -6 to 6
- key_y: bfloat16 [96, 128], P('traj'), parts along dimension 0, may hold values from -6 to 6
Outputs:
- grad_values: bfloat16 [64, 24, 128], P(('traj', 'slab')), parts along dimension 0
- query_x_grad: float32 [64, 128], P(('traj', 'slab')), parts along dimension 0
- key_x_grad: float32 [64, 128], P(('traj', 'slab')), parts along dimension 0
- query_y_grad: float32 [96, 128], P(('traj', 'slab')), parts along dimension 0
- key_y_grad: float32 [96, 128], P(('traj', 'slab')), parts along dimension 0
There are 4 independent parts, one for each index of `traj`. A program takes and returns all parts, laid end to end along the dimension named above; each array names one. Nothing has to cross between parts.
All inputs are finite; a program needn't handle non-finite values.
Results may differ from a plain program's by a relative error of at most 0.0067.
Values may be sent and summed in bfloat16 or wider, within the bound.
A program may use at most 64 MiB of HBM per device.

v0:
```python
import math

import jax
import jax.numpy as jnp
from jax import lax
from jax.sharding import PartitionSpec as P

HEADS = 4
HEAD = 32


def axis_kernel(queries, key_rows):
    scores = jnp.dot(queries, key_rows.T, preferred_element_type=jnp.float32) / math.sqrt(HEAD)
    return jax.nn.softmax(scores, axis=1)


def local_terms(kernel, coupling, queries, key_rows):
    row_delta = jnp.sum(kernel * coupling, axis=1)
    weighted = kernel * coupling
    grad_query = jnp.dot(
        weighted, key_rows.astype(jnp.float32), precision=lax.Precision.HIGHEST
    ) / math.sqrt(HEAD)
    grad_key = jnp.dot(
        weighted.T, queries.astype(jnp.float32), precision=lax.Precision.HIGHEST
    ) / math.sqrt(HEAD)
    return (grad_query, grad_key, row_delta)


def corrections(own_rows, own_cols, delta_total, queries, key_rows, start, count):
    own_delta = lax.dynamic_slice_in_dim(delta_total, start, count, 0)
    query_fix = (
        own_delta[:, None]
        * jnp.dot(own_rows, key_rows.astype(jnp.float32), precision=lax.Precision.HIGHEST)
        / math.sqrt(HEAD)
    )
    key_fix = jnp.dot(
        own_cols.T,
        delta_total[:, None] * queries.astype(jnp.float32),
        precision=lax.Precision.HIGHEST,
    ) / math.sqrt(HEAD)
    return (query_fix, key_fix)


def on_device(grad_out, cached, values, query_x, key_x, query_y, key_y):
    index = lax.axis_index("slab")
    x_rows = grad_out.shape[0]
    x_count = cached.shape[0]
    y_rows = cached.shape[1]
    x_start = index * x_rows
    y_start = index * y_rows
    grad_columns = lax.all_to_all(grad_out, "slab", split_axis=1, concat_axis=0, tiled=True)
    mixed_heads = []
    query_terms = []
    key_terms = []
    delta_terms = []
    row_slices = []
    col_slices = []
    for head_index in range(HEADS):
        offset = head_index * HEAD
        head_query = query_x[:, offset : offset + HEAD]
        head_key = key_x[:, offset : offset + HEAD]
        kernel = axis_kernel(head_query, head_key)
        grad_rows = grad_columns[:, :, offset : offset + HEAD].reshape(x_count, y_rows * HEAD)
        saved_rows = cached[:, :, offset : offset + HEAD].reshape(x_count, y_rows * HEAD)
        grad_mixed = lax.dot_general(
            kernel.astype(jnp.bfloat16),
            grad_rows,
            (((0,), (0,)), ((), ())),
            preferred_element_type=jnp.float32,
        ).astype(jnp.bfloat16)
        coupling = lax.dot_general(
            grad_rows, saved_rows, (((1,), (1,)), ((), ())), preferred_element_type=jnp.float32
        )
        grad_query, grad_key, row_delta = local_terms(kernel, coupling, head_query, head_key)
        query_terms.append(grad_query)
        key_terms.append(grad_key)
        delta_terms.append(row_delta)
        row_slices.append(lax.dynamic_slice_in_dim(kernel, x_start, x_rows, 0))
        col_slices.append(lax.dynamic_slice_in_dim(kernel, x_start, x_rows, 1))
        mixed_heads.append(grad_mixed.reshape(x_count, y_rows, HEAD))
    mixed_rows = lax.all_to_all(
        jnp.concatenate(mixed_heads, axis=2), "slab", split_axis=0, concat_axis=1, tiled=True
    )
    x_delta_total = lax.psum(jnp.stack(delta_terms), "slab")
    query_x_grad, key_x_grad = (
        lax.psum_scatter(
            jnp.concatenate(query_terms, axis=1), "slab", scatter_dimension=0, tiled=True
        ),
        lax.psum_scatter(
            jnp.concatenate(key_terms, axis=1), "slab", scatter_dimension=0, tiled=True
        ),
    )
    query_fixes = []
    key_fixes = []
    for head_index in range(HEADS):
        offset = head_index * HEAD
        query_fix, key_fix = corrections(
            row_slices[head_index],
            col_slices[head_index],
            x_delta_total[head_index],
            query_x[:, offset : offset + HEAD],
            key_x[:, offset : offset + HEAD],
            x_start,
            x_rows,
        )
        query_fixes.append(query_fix)
        key_fixes.append(key_fix)
    query_x_grad = query_x_grad - jnp.concatenate(query_fixes, axis=1)
    key_x_grad = key_x_grad - jnp.concatenate(key_fixes, axis=1)
    value_heads = []
    query_terms = []
    key_terms = []
    delta_terms = []
    row_slices = []
    col_slices = []
    for head_index in range(HEADS):
        offset = head_index * HEAD
        head_query = query_y[:, offset : offset + HEAD]
        head_key = key_y[:, offset : offset + HEAD]
        kernel = axis_kernel(head_query, head_key)
        mixed_head = mixed_rows[:, :, offset : offset + HEAD]
        value_head = values[:, :, offset : offset + HEAD]
        grad_value = jnp.einsum(
            "jk,xje->xke",
            kernel.astype(jnp.bfloat16),
            mixed_head,
            preferred_element_type=jnp.float32,
        )
        coupling = jnp.einsum(
            "xje,xke->jk", mixed_head, value_head, preferred_element_type=jnp.float32
        )
        grad_query, grad_key, row_delta = local_terms(kernel, coupling, head_query, head_key)
        query_terms.append(grad_query)
        key_terms.append(grad_key)
        delta_terms.append(row_delta)
        row_slices.append(lax.dynamic_slice_in_dim(kernel, y_start, y_rows, 0))
        col_slices.append(lax.dynamic_slice_in_dim(kernel, y_start, y_rows, 1))
        value_heads.append(grad_value.astype(jnp.bfloat16))
    y_delta_total = lax.psum(jnp.stack(delta_terms), "slab")
    query_y_grad, key_y_grad = (
        lax.psum_scatter(
            jnp.concatenate(query_terms, axis=1), "slab", scatter_dimension=0, tiled=True
        ),
        lax.psum_scatter(
            jnp.concatenate(key_terms, axis=1), "slab", scatter_dimension=0, tiled=True
        ),
    )
    query_fixes = []
    key_fixes = []
    for head_index in range(HEADS):
        offset = head_index * HEAD
        query_fix, key_fix = corrections(
            row_slices[head_index],
            col_slices[head_index],
            y_delta_total[head_index],
            query_y[:, offset : offset + HEAD],
            key_y[:, offset : offset + HEAD],
            y_start,
            y_rows,
        )
        query_fixes.append(query_fix)
        key_fixes.append(key_fix)
    query_y_grad = query_y_grad - jnp.concatenate(query_fixes, axis=1)
    key_y_grad = key_y_grad - jnp.concatenate(key_fixes, axis=1)
    grad_values = jnp.concatenate(value_heads, axis=2)
    return (grad_values, query_x_grad, key_x_grad, query_y_grad, key_y_grad)


def solution(mesh):
    return jax.shard_map(
        on_device,
        mesh=mesh,
        in_specs=(
            P(("traj", "slab"), None, None),
            P("traj", "slab", None),
            P(("traj", "slab"), None, None),
            P("traj", None),
            P("traj", None),
            P("traj", None),
            P("traj", None),
        ),
        out_specs=(
            P(("traj", "slab"), None, None),
            P(("traj", "slab"), None),
            P(("traj", "slab"), None),
            P(("traj", "slab"), None),
            P(("traj", "slab"), None),
        ),
        check_vma=False,
    )
```

profile of v0, /device:TPU:0, one launch (start us, length us, event | category | flops | bytes accessed | tf_op | source)
XLA Modules:
  0.0 65.9 jit_solution(17512728886956750238)
XLA Ops:
  0.6 1.3 %copy.25 = bf16[2,24,128]{2,0,1:T(2,128)(2,1)} copy(bf16[2,24,128]{2,1,0:T(8,128)(2,1)} %param.7) | data formatting | bytes 24576 | tf_op args[0]
  2.0 6.5 %all-to-all-start = ((bf16[2,24,128]{2,0,1:T(2,128)(2,1)}), bf16[2,24,128]{2,0,1:T(2,128)(2,1)S(1)}, u32[]{:S(2)}, u32[]{:S(2)}) async-start(bf16[2,24,128]{2,0,1:T(2,128)(2,1)} %copy.25), calls=%async_computation | async-start | bytes 24576 | tf_op jit(solution)/shard_map/all_to_all | solution.py:51
  9.2 0.5 copy-done
  10.9 0.6 copy-done.6
  11.6 0.6 dynamic-slice.8
  13.5 0.6 all-to-all-done
  14.1 0.6 copy-done.5
  18.4 0.7 %pad_maximum_fusion = bf16[16,3,128]{2,1,0:T(4,128)(2,1)} fusion(bf16[16,3,32]{2,1,0:T(4,128)(2,1)S(1)} %reshape.93, bf16[16,3,32]{2,1,0:T(4,128)(2,1)S(1)} %reshape.91, bf16[16,3,32]{2,1,0:T(4,128)(2,1)S(1)} %reshape.89, bf16[16,3,32]{2,1,0:T(4,128)(2,1)S(1)} %reshape.87), kind=kLoop, calls=%fused_computation.76 | loop fusion | flops 49152 | bytes 24576 | tf_op jit(solution)/shard_map/concatenate | solution.py:82
  19.1 4.5 %all-to-all-start.1 = ((bf16[16,3,128]{2,1,0:T(4,128)(2,1)}), bf16[16,3,128]{2,1,0:T(4,128)(2,1)S(1)}, u32[]{:S(2)}, u32[]{:S(2)}) async-start(bf16[16,3,128]{2,1,0:T(4,128)(2,1)} %pad_maximum_fusion), calls=%async_computation.1 | async-start | bytes 32768 | tf_op jit(solution)/shard_map/all_to_all | solution.py:81
  23.8 5.5 %all-to-all-done.1 = bf16[16,3,128]{2,1,0:T(4,128)(2,1)S(1)} async-done(((bf16[16,3,128]{2,1,0:T(4,128)(2,1)}), bf16[16,3,128]{2,1,0:T(4,128)(2,1)S(1)}, u32[]{:S(2)}, u32[]{:S(2)}) %all-to-all-start.1) | async-done | bytes 12320 | tf_op jit(solution)/shard_map/all_to_all | solution.py:81
  29.5 0.6 copy-done.4
  33.0 26.4 %all-reduce.4 = (f32[16,128]{1,0:T(8,128)S(1)}, f32[4,16]{1,0:T(4,128)S(1)}, f32[16,128]{1,0:T(8,128)S(1)}, f32[4,24]{1,0:T(4,128)S(1)}, f32[24,128]{1,0:T(8,128)S(1)}, /*index=5*/f32[24,128]{1,0:T(8,128)S(1)}) all-reduce(f32[16,128]{1,0:T(8,128)S(1)} %pad_maximum_fusion.4, ...), channel_id=2, replica_groups=mesh['traj'=4,'slab'=8] {'slab'}, use_global_device_ids=true, to_apply=%region_16.0.clone | all-reduce | flops 10400 | bytes 83200
  59.6 0.2 fusion.16
  60.2 0.2 fusion.18
  60.5 0.2 fusion.19
  60.7 0.3 convolution_multiply_fusion.32
  61.8 0.2 fusion.12
  62.1 0.2 fusion.13
  62.4 0.2 fusion.14
  62.7 0.3 fusion.15
  63.0 0.3 convolution_multiply_fusion.24
  63.9 0.7 %pad_maximum_fusion.1 = bf16[2,24,128]{2,1,0:T(8,128)(2,1)} fusion(bf16[2,24,32]{2,1,0:T(8,128)(2,1)S(1)} %fusion.3, bf16[2,24,32]{2,1,0:T(8,128)(2,1)S(1)} %fusion.2, bf16[2,24,32]{2,1,0:T(8,128)(2,1)S(1)} %fusion.1, bf16[2,24,32]{2,1,0:T(8,128)(2,1)S(1)} %fusion), kind=kLoop, calls=%fused_computation.77 | loop fusion | flops 49152 | bytes 24576 | tf_op jit(solution)/shard_map/concatenate | solution.py:165
  64.6 0.6 fusion.152
  65.2 0.7 %maximum_subtract_fusion = (f32[3,128]{1,0:T(4,128)}, f32[3,128]{1,0:T(4,128)}) fusion(f32[3,32]{1,0:T(4,128)S(1)} %fusion.12, f32[3,32]{1,0:T(4,128)S(1)} %fusion.13, f32[3,32]{1,0:T(4,128)S(1)} %fusion.14, f32[3,32]{1,0:T(4,128)S(1)} %fusion.15, f32[24,128]{1,0:T(8,128)S(1)} %get-tuple-element.9, u32[]{:T(128)S(6)} %multiply.45, ...), kind=kLoop, calls=%fused_computation.240 | loop fusion | flops 3072 | bytes 9220 | tf_op jit(solution)/shard_map/sub | solution.py:163
  (105 shorter events, 10.9 us)
Async XLA Ops:
  1.9 6.5 %copy-start.2 = (bf16[16,128]{1,0:T(8,128)(2,1)S(1)}, bf16[16,128]{1,0:T(8,128)(2,1)}, u32[]{:S(2)}) copy-start(bf16[16,128]{1,0:T(8,128)(2,1)} %param.11) | copy-start | bytes 12292
  1.9 6.5 %copy-start.3 = (bf16[16,128]{1,0:T(8,128)(2,1)S(1)}, bf16[16,128]{1,0:T(8,128)(2,1)}, u32[]{:S(2)}) copy-start(bf16[16,128]{1,0:T(8,128)(2,1)} %param.10) | copy-start | bytes 12292
  2.0 12.1 %all-to-all-start = ((bf16[2,24,128]{2,0,1:T(2,128)(2,1)}), bf16[2,24,128]{2,0,1:T(2,128)(2,1)S(1)}, u32[]{:S(2)}, u32[]{:S(2)}) async-start(bf16[2,24,128]{2,0,1:T(2,128)(2,1)} %copy.25), calls=%async_computation | async-start | bytes 24576 | tf_op jit(solution)/shard_map/all_to_all | solution.py:51
  9.0 0.7 %copy-start = (bf16[24,128]{1,0:T(8,128)(2,1)S(1)}, bf16[24,128]{1,0:T(8,128)(2,1)}, u32[]{:S(2)}) copy-start(bf16[24,128]{1,0:T(8,128)(2,1)} %param.13) | copy-start | bytes 18436
  9.1 0.7 %copy-start.1 = (bf16[24,128]{1,0:T(8,128)(2,1)S(1)}, bf16[24,128]{1,0:T(8,128)(2,1)}, u32[]{:S(2)}) copy-start(bf16[24,128]{1,0:T(8,128)(2,1)} %param.12) | copy-start | bytes 18436
  10.9 0.7 %copy-start.6 = (u32[32]{0:T(128)S(1)}, u32[32]{0:T(128)}, u32[]{:S(2)}) copy-start(u32[32]{0:T(128)} %constant.80) | copy-start | bytes 388
  14.1 0.7 %copy-start.5 = (bf16[16,3,128]{2,0,1:T(8,128)(2,1)S(1)}, bf16[16,3,128]{2,0,1:T(8,128)(2,1)}, u32[]{:S(2)}) copy-start(bf16[16,3,128]{2,0,1:T(8,128)(2,1)} %param.8) | copy-start | bytes 36868
  19.1 10.2 %all-to-all-start.1 = ((bf16[16,3,128]{2,1,0:T(4,128)(2,1)}), bf16[16,3,128]{2,1,0:T(4,128)(2,1)S(1)}, u32[]{:S(2)}, u32[]{:S(2)}) async-start(bf16[16,3,128]{2,1,0:T(4,128)(2,1)} %pad_maximum_fusion), calls=%async_computation.1 | async-start | bytes 32768 | tf_op jit(solution)/shard_map/all_to_all | solution.py:81
  29.4 0.7 %copy-start.4 = (bf16[2,24,128]{2,1,0:T(8,128)(2,1)S(1)}, bf16[2,24,128]{2,1,0:T(8,128)(2,1)}, u32[]{:S(2)}) copy-start(bf16[2,24,128]{2,1,0:T(8,128)(2,1)} %param.9) | copy-start | bytes 36868
where the time goes:
time: 66.4 us; the launch traced here: 65.9 us
  blocking collectives  26.4 us (40%)
  starting transfers between devices  11 us (17%)
  matrix products  10.9 us (16%)
  waiting for transfers between devices  6.07 us (9%)
  local copies, waits for them, and re-layouts  5.88 us (9%)
  other arithmetic  3.34 us (5%)
  between operations  2.25 us (3%)
    unnamed x1, blocking collectives  26.4 us
    all_to_all x1, starting transfers between devices, on_device(): lax.all_to_all(grad_out, 'slab', split_axis=1, concat_axis=0, tiled=True)  6.46 us
    all_to_all x1, waiting for transfers between devices, on_device(): lax.all_to_all(jnp.concatenate(mixed_heads, axis=2), 'slab', split_axis=0...  5.48 us
    all_to_all x1, starting transfers between devices, on_device(): lax.all_to_all(jnp.concatenate(mixed_heads, axis=2), 'slab', split_axis=0...  4.52 us
    unnamed x16, local copies, waits for them, and re-layouts  4.32 us
    dot_general x8, matrix products, corrections(): jnp.dot(own_rows, key_rows.astype(jnp.float32), precision=lax.Precision.H...  1.92 us
    dot_general x8, matrix products, corrections(): jnp.dot(own_cols.T, delta_total[:, None] * queries.astype(jnp.float32), p...  1.81 us
    dot_general x8, matrix products, local_terms(): jnp.dot(weighted.T, queries.astype(jnp.float32), precision=lax.Precision....  1.57 us
  transfers between devices with their start and end apart: 2, of which 2 were waited for; matrix products, arithmetic and copies ran while one was open for 4% of the time, Pallas kernels for 0%

commit v1 on v0

--- a/solution.py
+++ b/solution.py
@@ -1,12 +1,16 @@
+import functools
 import math
 
 import jax
 import jax.numpy as jnp
 from jax import lax
+from jax.experimental import pallas as pl
+from jax.experimental.pallas import tpu as pltpu
 from jax.sharding import PartitionSpec as P
 
 HEADS = 4
 HEAD = 32
+CHANNELS = HEADS * HEAD
 
 
 def axis_kernel(queries, key_rows):
@@ -41,7 +45,7 @@
     return (query_fix, key_fix)
 
 
-def on_device(grad_out, cached, values, query_x, key_x, query_y, key_y):
+def exchanged_form(grad_out, cached, values, query_x, key_x, query_y, key_y):
     index = lax.axis_index("slab")
     x_rows = grad_out.shape[0]
     x_count = cached.shape[0]
@@ -166,9 +170,254 @@
     return (grad_values, query_x_grad, key_x_grad, query_y_grad, key_y_grad)
 
 
+def gather_kernel(
+    n,
+    grad_hbm,
+    cached_ref,
+    values_ref,
+    query_x_ref,
+    key_x_ref,
+    query_y_ref,
+    key_y_ref,
+    grad_values_ref,
+    query_x_grad_ref,
+    key_x_grad_ref,
+    query_y_grad_ref,
+    key_y_grad_ref,
+    gathered,
+    wide,
+    outgoing,
+    incoming,
+    own_sem,
+    gather_send,
+    gather_recv,
+    term_send,
+    term_recv,
+):
+    me = lax.axis_index("slab")
+    peers = [lax.rem(me + step, n) for step in range(1, n)]
+    x_rows, y_count = values_ref.shape[0], values_ref.shape[1]
+    x_count, y_rows = cached_ref.shape[0], cached_ref.shape[1]
+    scale = 1.0 / math.sqrt(HEAD)
+
+    own = pltpu.make_async_copy(grad_hbm, gathered.at[me], own_sem)
+    own.start()
+    barrier = pltpu.get_barrier_semaphore()
+    for peer in peers:
+        pl.semaphore_signal(barrier, inc=1, device_id={"slab": peer}, device_id_type=MESH)
+    pl.semaphore_wait(barrier, n - 1)
+    gathers = []
+    for peer in reversed(peers):
+        copy = pltpu.make_async_remote_copy(
+            src_ref=grad_hbm,
+            dst_ref=gathered.at[me],
+            send_sem=gather_send.at[peer],
+            recv_sem=gather_recv.at[me],
+            device_id={"slab": peer},
+            device_id_type=MESH,
+        )
+        copy.start()
+        gathers.append(copy)
+
+    query_x, kernel_x = masked_kernel(query_x_ref[...], key_x_ref[...])
+    query_y, kernel_y = masked_kernel(query_y_ref[...], key_y_ref[...])
+    width = x_rows * CHANNELS
+    rows = lax.broadcasted_iota(jnp.int32, (x_count, width), 0)
+    lanes = lax.broadcasted_iota(jnp.int32, (x_count, width), 1)
+    own_columns = (rows == me * x_rows + lanes // CHANNELS).astype(jnp.bfloat16)
+    spread = per_head_sum(
+        jnp.dot(
+            kernel_x.astype(jnp.bfloat16), own_columns, preferred_element_type=jnp.float32
+        )
+    )
+    kernel_y_low = kernel_y.astype(jnp.bfloat16)
+    cached = cached_ref[...].astype(jnp.float32)
+    saved = jnp.concatenate(
+        [cached[:, y, :] for y in range(y_rows)], axis=1
+    ).astype(jnp.bfloat16)
+    values = jnp.concatenate([values_ref[x] for x in range(x_rows)], axis=1)
+
+    own.wait()
+    for peer in peers:
+        pltpu.make_async_remote_copy(
+            src_ref=grad_hbm,
+            dst_ref=gathered.at[peer],
+            send_sem=gather_send.at[peer],
+            recv_sem=gather_recv.at[peer],
+            device_id={"slab": peer},
+            device_id_type=MESH,
+        ).wait_recv()
+
+    mixed = [jnp.zeros((y_count, CHANNELS), jnp.float32) for _ in range(x_rows)]
+    for slot in range(n):
+        block = gathered[slot].astype(jnp.float32)
+        wide[pl.ds(slot * x_rows * y_count, x_rows * y_count), :] = block
+        for r in range(x_rows):
+            i = slot * x_rows + r
+            row = block[r * y_count : (r + 1) * y_count, :]
+            for x in range(x_rows):
+                mixed[x] += row * spread[i : i + 1, x * CHANNELS : (x + 1) * CHANNELS]
+    grad_columns = jnp.concatenate(
+        [
+            wide[pl.ds(me * y_rows + y, x_count, stride=y_count), :]
+            for y in range(y_rows)
+        ],
+        axis=1,
+    )
+    mixed = jnp.concatenate(mixed, axis=1).astype(jnp.bfloat16).astype(jnp.float32)
+    mixed_heads = by_head(mixed)
+    coupling_x = lax.dot_general(
+        by_head(grad_columns), saved, ROWS_BY_ROWS, preferred_element_type=jnp.float32
+    )
+    coupling_y = lax.dot_general(
+        mixed_heads, values, ROWS_BY_ROWS, preferred_element_type=jnp.float32
+    )
+    query_x_term, key_x_term = factor_terms(kernel_x, coupling_x, query_x, key_x_ref[...])
+    query_y_term, key_y_term = factor_terms(kernel_y, coupling_y, query_y, key_y_ref[...])
+    for slot in range(n):
+        outgoing[slot, 0:x_rows, :] = query_x_term[slot * x_rows : (slot + 1) * x_rows]
+        outgoing[slot, x_rows : 2 * x_rows, :] = key_x_term[slot * x_rows : (slot + 1) * x_rows]
+        start = 2 * x_rows
+        outgoing[slot, start : start + y_rows, :] = query_y_term[slot * y_rows : (slot + 1) * y_rows]
+        start += y_rows
+        outgoing[slot, start : start + y_rows, :] = key_y_term[slot * y_rows : (slot + 1) * y_rows]
+    terms = []
+    for peer in reversed(peers):
+        copy = pltpu.make_async_remote_copy(
+            src_ref=outgoing.at[peer],
+            dst_ref=incoming.at[me],
+            send_sem=term_send.at[peer],
+            recv_sem=term_recv.at[me],
+            device_id={"slab": peer},
+            device_id_type=MESH,
+        )
+        copy.start()
+        terms.append(copy)
+
+    grad_values = lax.dot_general(
+        kernel_y_low,
+        mixed_heads,
+        COLUMNS_BY_COLUMNS,
+        preferred_element_type=jnp.float32,
+    ).astype(grad_values_ref.dtype)
+    for x in range(x_rows):
+        grad_values_ref[x] = grad_values[:, x * CHANNELS : (x + 1) * CHANNELS]
+
+    total = outgoing[me]
+    for peer in peers:
+        pltpu.make_async_remote_copy(
+            src_ref=outgoing.at[peer],
+            dst_ref=incoming.at[peer],
+            send_sem=term_send.at[peer],
+            recv_sem=term_recv.at[peer],
+            device_id={"slab": peer},
+            device_id_type=MESH,
+        ).wait_recv()
+        total += incoming[peer]
+    total *= scale
+    query_x_grad_ref[...] = total[0:x_rows]
+    key_x_grad_ref[...] = total[x_rows : 2 * x_rows]
+    query_y_grad_ref[...] = total[2 * x_rows : 2 * x_rows + y_rows]
+    key_y_grad_ref[...] = total[2 * x_rows + y_rows : 2 * x_rows + 2 * y_rows]
+    for copy in gathers + terms:
+        copy.wait_send()
+
+
+MESH = pl.DeviceIdType.MESH
+ROWS_BY_ROWS = (((1,), (1,)), ((), ()))
+COLUMNS_BY_COLUMNS = (((0,), (0,)), ((), ()))
+
+
+def by_head(array):
+    lanes = lax.broadcasted_iota(jnp.int32, array.shape, 1) % CHANNELS // HEAD
+    return jnp.concatenate(
+        [jnp.where(lanes == head, array, 0.0) for head in range(HEADS)], axis=0
+    ).astype(jnp.bfloat16)
+
+
+def per_head_sum(array):
+    rows = array.shape[0] // HEADS
+    lanes = lax.broadcasted_iota(jnp.int32, (rows, array.shape[1]), 1) % CHANNELS // HEAD
+    total = array[:rows]
+    for head in range(1, HEADS):
+        total = jnp.where(lanes == head, array[head * rows : (head + 1) * rows], total)
+    return total
+
+
+def masked_kernel(queries, key_rows):
+    heads = by_head(queries.astype(jnp.float32))
+    scores = lax.dot_general(
+        heads, key_rows, ROWS_BY_ROWS, preferred_element_type=jnp.float32
+    ) / math.sqrt(HEAD)
+    weights = jnp.exp(scores - jnp.max(scores, axis=1, keepdims=True))
+    return heads, weights / jnp.sum(weights, axis=1, keepdims=True)
+
+
+def factor_terms(kernel, coupling, queries, key_rows):
+    delta = jnp.sum(kernel * coupling, axis=1, keepdims=True)
+    weighted = kernel * (coupling - delta)
+    high = weighted.astype(jnp.bfloat16)
+    low = (weighted - high.astype(jnp.float32)).astype(jnp.bfloat16)
+    query_term = jnp.dot(high, key_rows, preferred_element_type=jnp.float32) + jnp.dot(
+        low, key_rows, preferred_element_type=jnp.float32
+    )
+    key_term = lax.dot_general(
+        high, queries, COLUMNS_BY_COLUMNS, preferred_element_type=jnp.float32
+    ) + lax.dot_general(low, queries, COLUMNS_BY_COLUMNS, preferred_element_type=jnp.float32)
+    return per_head_sum(query_term), key_term
+
+
+def gathered_form(n, grad_out, cached, values, query_x, key_x, query_y, key_y):
+    x_rows, y_count = grad_out.shape[:2]
+    x_count, y_rows = cached.shape[:2]
+    term_rows = -(-2 * (x_rows + y_rows) // 8) * 8
+    vmem = pl.BlockSpec(memory_space=pltpu.VMEM)
+    return pl.pallas_call(
+        functools.partial(gather_kernel, n),
+        out_shape=(
+            jax.ShapeDtypeStruct(values.shape, values.dtype),
+            jax.ShapeDtypeStruct((x_rows, CHANNELS), jnp.float32),
+            jax.ShapeDtypeStruct((x_rows, CHANNELS), jnp.float32),
+            jax.ShapeDtypeStruct((y_rows, CHANNELS), jnp.float32),
+            jax.ShapeDtypeStruct((y_rows, CHANNELS), jnp.float32),
+        ),
+        in_specs=[pl.BlockSpec(memory_space=pltpu.HBM)] + [vmem] * 6,
+        out_specs=(vmem,) * 5,
+        scratch_shapes=[
+            pltpu.VMEM((n, x_rows * y_count, CHANNELS), jnp.bfloat16),
+            pltpu.VMEM((x_count * y_count, CHANNELS), jnp.float32),
+            pltpu.VMEM((n, term_rows, CHANNELS), jnp.float32),
+            pltpu.VMEM((n, term_rows, CHANNELS), jnp.float32),
+            pltpu.SemaphoreType.DMA,
+            pltpu.SemaphoreType.DMA((n,)),
+            pltpu.SemaphoreType.DMA((n,)),
+            pltpu.SemaphoreType.DMA((n,)),
+            pltpu.SemaphoreType.DMA((n,)),
+        ],
+        compiler_params=pltpu.CompilerParams(collective_id=0, has_side_effects=True),
+    )(
+        grad_out.reshape(x_rows * y_count, CHANNELS),
+        cached,
+        values,
+        query_x,
+        key_x,
+        query_y,
+        key_y,
+    )
+
+
+GATHERED_BYTES = 1 << 20
+
+
+def on_device(n, *arrays):
+    if n > 1 and arrays[0].size * arrays[0].dtype.itemsize * n <= GATHERED_BYTES:
+        return gathered_form(n, *arrays)
+    return exchanged_form(*arrays)
+
+
 def solution(mesh):
     return jax.shard_map(
-        on_device,
+        functools.partial(on_device, mesh.shape["slab"]),
         mesh=mesh,
         in_specs=(
             P(("traj", "slab"), None, None),

time: 66.4 us -> 21.4 us (0.32)
  blocking collectives: 26.4 us -> 0 us
  Pallas kernels: 0 us -> 15.3 us
  starting transfers between devices: 11 us -> 0 us
  matrix products: 10.9 us -> 0 us
  waiting for transfers between devices: 6.07 us -> 0 us
  other arithmetic: 3.34 us -> 0 us
  between operations: 2.25 us -> 0.66 us
  local copies, waits for them, and re-layouts: 5.88 us -> 5 us
    unnamed x1 -> x0, blocking collectives: 26.4 us -> none
    pallas_call x0 -> x1, Pallas kernels: none -> 15.3 us  [gathered_form(): pl.pallas_call(functools.partial(gather_kernel, n), out_shape=(jax.ShapeD...]
    all_to_all x2 -> x0, starting transfers between devices: 11 us -> none  [the longest x1 6.46 us: on_device(): lax.all_to_all(grad_out, 'slab', split_axis=1, concat_axis=0, tiled=True)]
    dot_general x56 -> x0, matrix products: 10.9 us -> none  [the longest x8 1.92 us: corrections(): jnp.dot(own_rows, key_rows.astype(jnp.float32), precision=lax.Precision.H...]
    all_to_all x2 -> x0, waiting for transfers between devices: 6.07 us -> none  [the longest x1 5.48 us: on_device(): lax.all_to_all(jnp.concatenate(mixed_heads, axis=2), 'slab', split_axis=0...]
    concatenate x6 -> x0, other arithmetic: 1.72 us -> none  [the longest x1 0.7 us: on_device(): jnp.concatenate(mixed_heads, axis=2)]
    sub x2 -> x0, other arithmetic: 1.3 us -> none  [the longest x1 0.66 us: on_device(): query_y_grad = query_y_grad - jnp.concatenate(query_fixes, axis=1)]
    reshape x8 -> x0, local copies, waits for them, and re-layouts: 0.69 us -> none  [the longest x4 0.35 us: on_device(): grad_columns[:, :, offset:offset + HEAD].reshape(x_count, y_rows * HEAD)]
  transfers between devices with their start and end apart: 2 -> 0, of which waited for: 2 -> 0; matrix products, arithmetic and copies ran while one was open for 4% -> 0% of each run, Pallas kernels for 0% -> 0%
where the time goes in v1:
time: 21.4 us; the launch traced here: 21 us
  Pallas kernels  15.3 us (71%)
  local copies, waits for them, and re-layouts  5 us (23%)
  between operations  0.66 us (3%)
    pallas_call x1, Pallas kernels, gathered_form(): pl.pallas_call(functools.partial(gather_kernel, n), out_shape=(jax.ShapeD...  15.3 us
    unnamed x14, local copies, waits for them, and re-layouts  5 us

profile of v1, /device:TPU:0, one launch (start us, length us, event | category | flops | bytes accessed | tf_op | source)
XLA Modules:
  0.0 21.0 jit_solution(16730381331957451463)
XLA Ops:
  0.6 1.3 %copy.12.cached_ref = bf16[16,3,128]{2,1,0:T(4,128)(2,1)} copy(bf16[16,3,128]{2,0,1:T(8,128)(2,1)} %param.8) | data formatting | bytes 24576 | tf_op args[1]
  1.9 15.3 %shard_map.110 = (bf16[2,24,128]{2,1,0:T(8,128)(2,1)}, f32[2,128]{1,0:T(2,128)}, f32[2,128]{1,0:T(2,128)}, f32[3,128]{1,0:T(4,128)}, f32[3,128]{1,0:T(4,128)}) custom-call(bf16[48,128]{1,0:T(8,128)(2,1)} %bitcast.1, bf16[16,3,128]{2,1,0:T(4,128)(2,1)} %copy.12.cached_ref, bf16[2,24,128]{2,1,0:T(8,128)(2,1)} %values_ref.1, bf16[16,128]{1,0:T(8,128)(2,1)} %query_x_ref.1, ...), custom_call_target="tpu_custom_call" | custom-call | tf_op jit(solution)/shard_map/pallas_call | solution.py:375
  17.3 0.0 copy-start.3
  17.3 0.0 copy-start.2
  17.3 1.3 %copy.18 = bf16[2,24,128]{2,1,0:T(8,128)(2,1)} copy(bf16[2,24,128]{2,1,0:T(8,128)(2,1)} %get-tuple-element.10) | data formatting | bytes 24576
  18.6 0.0 copy-done.3
  18.6 0.0 copy-start.1
  18.6 0.6 %copy.19 = f32[2,128]{1,0:T(2,128)} copy(f32[2,128]{1,0:T(2,128)S(1)} %copy-done.3) | data formatting | bytes 2048
  19.2 0.0 copy-done.2
  19.2 0.6 %copy.20 = f32[2,128]{1,0:T(2,128)} copy(f32[2,128]{1,0:T(2,128)S(1)} %copy-done.2) | data formatting | bytes 2048
  19.7 0.0 copy-done.1
  19.7 0.0 copy-start
  19.7 0.6 %copy.21 = f32[3,128]{1,0:T(4,128)} copy(f32[3,128]{1,0:T(4,128)S(1)} %copy-done.1) | data formatting | bytes 3072
  20.3 0.1 copy-done
  20.4 0.6 %copy.22 = f32[3,128]{1,0:T(4,128)} copy(f32[3,128]{1,0:T(4,128)S(1)} %copy-done) | data formatting | bytes 3072
Async XLA Ops:
  17.3 1.3 %copy-start.3 = (f32[2,128]{1,0:T(2,128)S(1)}, f32[2,128]{1,0:T(2,128)}, u32[]{:S(2)}) copy-start(f32[2,128]{1,0:T(2,128)} %get-tuple-element.11) | copy-start | bytes 3076
  17.3 1.9 %copy-start.2 = (f32[2,128]{1,0:T(2,128)S(1)}, f32[2,128]{1,0:T(2,128)}, u32[]{:S(2)}) copy-start(f32[2,128]{1,0:T(2,128)} %get-tuple-element.12) | copy-start | bytes 3076
  18.6 1.1 %copy-start.1 = (f32[3,128]{1,0:T(4,128)S(1)}, f32[3,128]{1,0:T(4,128)}, u32[]{:S(2)}) copy-start(f32[3,128]{1,0:T(4,128)} %get-tuple-element.13) | copy-start | bytes 4612
  19.7 0.7 %copy-start = (f32[3,128]{1,0:T(4,128)S(1)}, f32[3,128]{1,0:T(4,128)}, u32[]{:S(2)}) copy-start(f32[3,128]{1,0:T(4,128)} %get-tuple-element.14) | copy-start | bytes 4612

commit v2 on v1

--- a/solution.py
+++ b/solution.py
@@ -170,25 +170,34 @@
     return (grad_values, query_x_grad, key_x_grad, query_y_grad, key_y_grad)
 
 
+MESH = pl.DeviceIdType.MESH
+ROWS_BY_ROWS = (((1,), (1,)), ((), ()))
+
+
 def gather_kernel(
     n,
+    x_rows,
+    y_rows,
     grad_hbm,
+    cached_hbm,
+    values_hbm,
+    query_x_hbm,
+    key_x_hbm,
+    query_y_hbm,
+    key_y_hbm,
+    grad_values_ref,
+    factors_ref,
+    gathered,
     cached_ref,
     values_ref,
     query_x_ref,
     key_x_ref,
     query_y_ref,
     key_y_ref,
-    grad_values_ref,
-    query_x_grad_ref,
-    key_x_grad_ref,
-    query_y_grad_ref,
-    key_y_grad_ref,
-    gathered,
     wide,
     outgoing,
     incoming,
-    own_sem,
+    own_sems,
     gather_send,
     gather_recv,
     term_send,
@@ -196,15 +205,26 @@
 ):
     me = lax.axis_index("slab")
     peers = [lax.rem(me + step, n) for step in range(1, n)]
-    x_rows, y_count = values_ref.shape[0], values_ref.shape[1]
-    x_count, y_rows = cached_ref.shape[0], cached_ref.shape[1]
-    scale = 1.0 / math.sqrt(HEAD)
-
-    own = pltpu.make_async_copy(grad_hbm, gathered.at[me], own_sem)
-    own.start()
+    x_count, y_count = query_x_ref.shape[0], query_y_ref.shape[0]
+
     barrier = pltpu.get_barrier_semaphore()
     for peer in peers:
         pl.semaphore_signal(barrier, inc=1, device_id={"slab": peer}, device_id_type=MESH)
+    own_pairs = (
+        (query_x_hbm, query_x_ref),
+        (key_x_hbm, key_x_ref),
+        (query_y_hbm, query_y_ref),
+        (key_y_hbm, key_y_ref),
+        (grad_hbm, gathered.at[me]),
+        (cached_hbm, cached_ref),
+        (values_hbm, values_ref),
+    )
+    own = [
+        pltpu.make_async_copy(source, target, own_sems.at[place])
+        for place, (source, target) in enumerate(own_pairs)
+    ]
+    for copy in own:
+        copy.start()
     pl.semaphore_wait(barrier, n - 1)
     gathers = []
     for peer in reversed(peers):
@@ -219,25 +239,32 @@
         copy.start()
         gathers.append(copy)
 
-    query_x, kernel_x = masked_kernel(query_x_ref[...], key_x_ref[...])
-    query_y, kernel_y = masked_kernel(query_y_ref[...], key_y_ref[...])
+    for copy in own:
+        copy.wait()
+    key_x, key_y = key_x_ref[...], key_y_ref[...]
+    query_x = by_head(query_x_ref[...].astype(jnp.float32))
+    query_y = by_head(query_y_ref[...].astype(jnp.float32))
+    kernel_x, kernel_x_turned = both_kernels(query_x, key_x)
+    kernel_y, kernel_y_turned = both_kernels(query_y, key_y)
     width = x_rows * CHANNELS
     rows = lax.broadcasted_iota(jnp.int32, (x_count, width), 0)
     lanes = lax.broadcasted_iota(jnp.int32, (x_count, width), 1)
     own_columns = (rows == me * x_rows + lanes // CHANNELS).astype(jnp.bfloat16)
-    spread = per_head_sum(
+    spread = per_head(
         jnp.dot(
             kernel_x.astype(jnp.bfloat16), own_columns, preferred_element_type=jnp.float32
         )
     )
-    kernel_y_low = kernel_y.astype(jnp.bfloat16)
+    kernel_y_low = kernel_y_turned.astype(jnp.bfloat16)
     cached = cached_ref[...].astype(jnp.float32)
-    saved = jnp.concatenate(
-        [cached[:, y, :] for y in range(y_rows)], axis=1
+    cached = jnp.concatenate(
+        [cached[y * x_count : (y + 1) * x_count] for y in range(y_rows)], axis=1
     ).astype(jnp.bfloat16)
-    values = jnp.concatenate([values_ref[x] for x in range(x_rows)], axis=1)
-
-    own.wait()
+    values = values_ref[...].astype(jnp.float32)
+    values = jnp.concatenate(
+        [values[x * y_count : (x + 1) * y_count] for x in range(x_rows)], axis=1
+    ).astype(jnp.bfloat16)
+
     for peer in peers:
         pltpu.make_async_remote_copy(
             src_ref=grad_hbm,
@@ -264,23 +291,24 @@
         ],
         axis=1,
     )
-    mixed = jnp.concatenate(mixed, axis=1).astype(jnp.bfloat16).astype(jnp.float32)
-    mixed_heads = by_head(mixed)
-    coupling_x = lax.dot_general(
-        by_head(grad_columns), saved, ROWS_BY_ROWS, preferred_element_type=jnp.float32
-    )
-    coupling_y = lax.dot_general(
-        mixed_heads, values, ROWS_BY_ROWS, preferred_element_type=jnp.float32
-    )
-    query_x_term, key_x_term = factor_terms(kernel_x, coupling_x, query_x, key_x_ref[...])
-    query_y_term, key_y_term = factor_terms(kernel_y, coupling_y, query_y, key_y_ref[...])
+    grad_columns = by_head(grad_columns)
+    mixed = by_head(jnp.concatenate(mixed, axis=1).astype(jnp.bfloat16).astype(jnp.float32))
+    query_x_term, key_x_term = factor_terms(
+        kernel_x, kernel_x_turned, grad_columns, cached, query_x, key_x
+    )
+    query_y_term, key_y_term = factor_terms(
+        kernel_y, kernel_y_turned, mixed, values, query_y, key_y
+    )
     for slot in range(n):
-        outgoing[slot, 0:x_rows, :] = query_x_term[slot * x_rows : (slot + 1) * x_rows]
-        outgoing[slot, x_rows : 2 * x_rows, :] = key_x_term[slot * x_rows : (slot + 1) * x_rows]
-        start = 2 * x_rows
-        outgoing[slot, start : start + y_rows, :] = query_y_term[slot * y_rows : (slot + 1) * y_rows]
-        start += y_rows
-        outgoing[slot, start : start + y_rows, :] = key_y_term[slot * y_rows : (slot + 1) * y_rows]
+        start = 0
+        for term, count in (
+            (query_x_term, x_rows),
+            (key_x_term, x_rows),
+            (query_y_term, y_rows),
+            (key_y_term, y_rows),
+        ):
+            outgoing[slot, start : start + count, :] = term[slot * count : (slot + 1) * count]
+            start += count
     terms = []
     for peer in reversed(peers):
         copy = pltpu.make_async_remote_copy(
@@ -294,14 +322,11 @@
         copy.start()
         terms.append(copy)
 
-    grad_values = lax.dot_general(
-        kernel_y_low,
-        mixed_heads,
-        COLUMNS_BY_COLUMNS,
-        preferred_element_type=jnp.float32,
-    ).astype(grad_values_ref.dtype)
+    grad_values = jnp.dot(kernel_y_low, mixed, preferred_element_type=jnp.float32)
     for x in range(x_rows):
-        grad_values_ref[x] = grad_values[:, x * CHANNELS : (x + 1) * CHANNELS]
+        grad_values_ref[x] = grad_values[:, x * CHANNELS : (x + 1) * CHANNELS].astype(
+            grad_values_ref.dtype
+        )
 
     total = outgoing[me]
     for peer in peers:
@@ -314,18 +339,9 @@
             device_id_type=MESH,
         ).wait_recv()
         total += incoming[peer]
-    total *= scale
-    query_x_grad_ref[...] = total[0:x_rows]
-    key_x_grad_ref[...] = total[x_rows : 2 * x_rows]
-    query_y_grad_ref[...] = total[2 * x_rows : 2 * x_rows + y_rows]
-    key_y_grad_ref[...] = total[2 * x_rows + y_rows : 2 * x_rows + 2 * y_rows]
+    factors_ref[...] = total * (1.0 / math.sqrt(HEAD))
     for copy in gathers + terms:
         copy.wait_send()
-
-
-MESH = pl.DeviceIdType.MESH
-ROWS_BY_ROWS = (((1,), (1,)), ((), ()))
-COLUMNS_BY_COLUMNS = (((0,), (0,)), ((), ()))
 
 
 def by_head(array):
@@ -335,60 +351,83 @@
     ).astype(jnp.bfloat16)
 
 
-def per_head_sum(array):
+def per_head(array):
     rows = array.shape[0] // HEADS
     lanes = lax.broadcasted_iota(jnp.int32, (rows, array.shape[1]), 1) % CHANNELS // HEAD
-    total = array[:rows]
+    picked = array[:rows]
     for head in range(1, HEADS):
-        total = jnp.where(lanes == head, array[head * rows : (head + 1) * rows], total)
-    return total
-
-
-def masked_kernel(queries, key_rows):
-    heads = by_head(queries.astype(jnp.float32))
-    scores = lax.dot_general(
-        heads, key_rows, ROWS_BY_ROWS, preferred_element_type=jnp.float32
-    ) / math.sqrt(HEAD)
-    weights = jnp.exp(scores - jnp.max(scores, axis=1, keepdims=True))
-    return heads, weights / jnp.sum(weights, axis=1, keepdims=True)
-
-
-def factor_terms(kernel, coupling, queries, key_rows):
-    delta = jnp.sum(kernel * coupling, axis=1, keepdims=True)
+        picked = jnp.where(lanes == head, array[head * rows : (head + 1) * rows], picked)
+    return picked
+
+
+def rows_by_rows(left, right):
+    return lax.dot_general(left, right, ROWS_BY_ROWS, preferred_element_type=jnp.float32)
+
+
+def both_kernels(queries, key_rows):
+    kernels = []
+    for scores, axis in (
+        (rows_by_rows(queries, key_rows), 1),
+        (rows_by_rows(key_rows, queries), 0),
+    ):
+        scores = scores / math.sqrt(HEAD)
+        weights = jnp.exp(scores - jnp.max(scores, axis=axis, keepdims=True))
+        kernels.append(weights / jnp.sum(weights, axis=axis, keepdims=True))
+    return kernels
+
+
+def weighted_parts(kernel, coupling, axis):
+    delta = jnp.sum(kernel * coupling, axis=axis, keepdims=True)
     weighted = kernel * (coupling - delta)
     high = weighted.astype(jnp.bfloat16)
-    low = (weighted - high.astype(jnp.float32)).astype(jnp.bfloat16)
+    return high, (weighted - high.astype(jnp.float32)).astype(jnp.bfloat16)
+
+
+def factor_terms(kernel, kernel_turned, left, right, queries, key_rows):
+    high, low = weighted_parts(kernel, rows_by_rows(left, right), 1)
     query_term = jnp.dot(high, key_rows, preferred_element_type=jnp.float32) + jnp.dot(
         low, key_rows, preferred_element_type=jnp.float32
     )
-    key_term = lax.dot_general(
-        high, queries, COLUMNS_BY_COLUMNS, preferred_element_type=jnp.float32
-    ) + lax.dot_general(low, queries, COLUMNS_BY_COLUMNS, preferred_element_type=jnp.float32)
-    return per_head_sum(query_term), key_term
+    high, low = weighted_parts(kernel_turned, rows_by_rows(right, left), 0)
+    key_term = jnp.dot(high, queries, preferred_element_type=jnp.float32) + jnp.dot(
+        low, queries, preferred_element_type=jnp.float32
+    )
+    return per_head(query_term), key_term
+
+
+def hand_out_kernel(values_ref, factors_ref, *out_refs):
+    out_refs[0][...] = values_ref[...]
+    start = 0
+    for out_ref in out_refs[1:]:
+        out_ref[...] = factors_ref[start : start + out_ref.shape[0], :]
+        start += out_ref.shape[0]
 
 
 def gathered_form(n, grad_out, cached, values, query_x, key_x, query_y, key_y):
     x_rows, y_count = grad_out.shape[:2]
     x_count, y_rows = cached.shape[:2]
-    term_rows = -(-2 * (x_rows + y_rows) // 8) * 8
+    term_rows = 2 * (x_rows + y_rows)
     vmem = pl.BlockSpec(memory_space=pltpu.VMEM)
-    return pl.pallas_call(
-        functools.partial(gather_kernel, n),
+    grad_values, factors = pl.pallas_call(
+        functools.partial(gather_kernel, n, x_rows, y_rows),
         out_shape=(
             jax.ShapeDtypeStruct(values.shape, values.dtype),
-            jax.ShapeDtypeStruct((x_rows, CHANNELS), jnp.float32),
-            jax.ShapeDtypeStruct((x_rows, CHANNELS), jnp.float32),
-            jax.ShapeDtypeStruct((y_rows, CHANNELS), jnp.float32),
-            jax.ShapeDtypeStruct((y_rows, CHANNELS), jnp.float32),
-        ),
-        in_specs=[pl.BlockSpec(memory_space=pltpu.HBM)] + [vmem] * 6,
-        out_specs=(vmem,) * 5,
+            jax.ShapeDtypeStruct((term_rows, CHANNELS), jnp.float32),
+        ),
+        in_specs=[pl.BlockSpec(memory_space=pltpu.HBM)] * 7,
+        out_specs=(vmem, vmem),
         scratch_shapes=[
             pltpu.VMEM((n, x_rows * y_count, CHANNELS), jnp.bfloat16),
+            pltpu.VMEM((y_rows * x_count, CHANNELS), jnp.bfloat16),
+            pltpu.VMEM((x_rows * y_count, CHANNELS), jnp.bfloat16),
+            pltpu.VMEM(query_x.shape, query_x.dtype),
+            pltpu.VMEM(key_x.shape, key_x.dtype),
+            pltpu.VMEM(query_y.shape, query_y.dtype),
+            pltpu.VMEM(key_y.shape, key_y.dtype),
             pltpu.VMEM((x_count * y_count, CHANNELS), jnp.float32),
             pltpu.VMEM((n, term_rows, CHANNELS), jnp.float32),
             pltpu.VMEM((n, term_rows, CHANNELS), jnp.float32),
-            pltpu.SemaphoreType.DMA,
+            pltpu.SemaphoreType.DMA((7,)),
             pltpu.SemaphoreType.DMA((n,)),
             pltpu.SemaphoreType.DMA((n,)),
             pltpu.SemaphoreType.DMA((n,)),
@@ -397,13 +436,21 @@
         compiler_params=pltpu.CompilerParams(collective_id=0, has_side_effects=True),
     )(
         grad_out.reshape(x_rows * y_count, CHANNELS),
-        cached,
-        values,
+        cached.transpose(1, 0, 2).reshape(y_rows * x_count, CHANNELS),
+        values.reshape(x_rows * y_count, CHANNELS),
         query_x,
         key_x,
         query_y,
         key_y,
     )
+    counts = (x_rows, x_rows, y_rows, y_rows)
+    return pl.pallas_call(
+        hand_out_kernel,
+        out_shape=(jax.ShapeDtypeStruct(values.shape, values.dtype),)
+        + tuple(jax.ShapeDtypeStruct((count, CHANNELS), jnp.float32) for count in counts),
+        in_specs=[vmem] * 2,
+        out_specs=(vmem,) * 5,
+    )(grad_values, factors)
 
 
 GATHERED_BYTES = 1 << 20

time: 21.4 us -> 16.7 us (0.78)
  local copies, waits for them, and re-layouts: 5 us -> 0 us
  Pallas kernels: 15.3 us -> 15.8 us
    unnamed x14 -> x0, local copies, waits for them, and re-layouts: 5 us -> none
    pallas_call x1 -> x2, Pallas kernels: 15.3 us -> 15.8 us  [the longest x1 14.4 us: gathered_form(): pl.pallas_call(functools.partial(gather_kernel, n, x_rows, y_rows), out_s...]
where the time goes in v2:
time: 16.7 us; the launch traced here: 16.4 us
  Pallas kernels  15.8 us (95%)
  between operations  0.64 us (4%)
    pallas_call x1, Pallas kernels, gathered_form(): pl.pallas_call(functools.partial(gather_kernel, n, x_rows, y_rows), out_s...  14.4 us
    pallas_call x1, Pallas kernels, gathered_form(): pl.pallas_call(hand_out_kernel, out_shape=(jax.ShapeDtypeStruct(values.sh...  1.33 us

profile of v2, /device:TPU:0, one launch (start us, length us, event | category | flops | bytes accessed | tf_op | source)
XLA Modules:
  0.0 16.4 jit_solution(6508902553918293089)
XLA Ops:
  0.6 14.4 %shard_map.110 = (bf16[2,24,128]{2,1,0:T(8,128)(2,1)}, f32[10,128]{1,0:T(8,128)}) custom-call(bf16[48,128]{1,0:T(8,128)(2,1)} %bitcast.5, bf16[48,128]{1,0:T(8,128)(2,1)} %bitcast.6, bf16[48,128]{1,0:T(8,128)(2,1)} %bitcast.7, bf16[16,128]{1,0:T(8,128)(2,1)} %query_x_hbm.1, bf16[16,128]{1,0:T(8,128)(2,1)} %key_x_hbm.1, bf16[24,128]{1,0:T(8,128)(2,1)} %query_y_hbm.1, ...), custom_call_target="tpu_custom_call" | custom-call | tf_op jit(solution)/shard_map/pallas_call | solution.py:411
  15.1 1.3 %shard_map.111 = (bf16[2,24,128]{2,1,0:T(8,128)(2,1)}, f32[2,128]{1,0:T(2,128)}, f32[2,128]{1,0:T(2,128)}, f32[3,128]{1,0:T(4,128)}, f32[3,128]{1,0:T(4,128)}) custom-call(bf16[2,24,128]{2,1,0:T(8,128)(2,1)} %get-tuple-element.7.values_ref, f32[10,128]{1,0:T(8,128)} %get-tuple-element.8.factors_ref), custom_call_target="tpu_custom_call" | custom-call | tf_op jit(solution)/shard_map/pallas_call | solution.py:447

commit v3 on v2

--- a/solution.py
+++ b/solution.py
@@ -194,6 +194,7 @@
     key_x_ref,
     query_y_ref,
     key_y_ref,
+    spread,
     wide,
     outgoing,
     incoming,
@@ -204,9 +205,13 @@
     term_recv,
 ):
     me = lax.axis_index("slab")
-    peers = [lax.rem(me + step, n) for step in range(1, n)]
+    peers = [
+        lax.rem(me + step, n) for step in sorted(range(1, n), key=lambda s: abs(2 * s - n))
+    ]
     x_count, y_count = query_x_ref.shape[0], query_y_ref.shape[0]
 
+    own_grad = pltpu.make_async_copy(grad_hbm, gathered.at[me], own_sems.at[6])
+    own_grad.start()
     barrier = pltpu.get_barrier_semaphore()
     for peer in peers:
         pl.semaphore_signal(barrier, inc=1, device_id={"slab": peer}, device_id_type=MESH)
@@ -215,7 +220,6 @@
         (key_x_hbm, key_x_ref),
         (query_y_hbm, query_y_ref),
         (key_y_hbm, key_y_ref),
-        (grad_hbm, gathered.at[me]),
         (cached_hbm, cached_ref),
         (values_hbm, values_ref),
     )
@@ -225,11 +229,12 @@
     ]
     for copy in own:
         copy.start()
+    own_grad.wait()
     pl.semaphore_wait(barrier, n - 1)
     gathers = []
-    for peer in reversed(peers):
+    for peer in peers:
         copy = pltpu.make_async_remote_copy(
-            src_ref=grad_hbm,
+            src_ref=gathered.at[me],
             dst_ref=gathered.at[me],
             send_sem=gather_send.at[peer],
             recv_sem=gather_recv.at[me],
@@ -250,7 +255,7 @@
     rows = lax.broadcasted_iota(jnp.int32, (x_count, width), 0)
     lanes = lax.broadcasted_iota(jnp.int32, (x_count, width), 1)
     own_columns = (rows == me * x_rows + lanes // CHANNELS).astype(jnp.bfloat16)
-    spread = per_head(
+    spread[...] = per_head(
         jnp.dot(
             kernel_x.astype(jnp.bfloat16), own_columns, preferred_element_type=jnp.float32
         )
@@ -265,25 +270,25 @@
         [values[x * y_count : (x + 1) * y_count] for x in range(x_rows)], axis=1
     ).astype(jnp.bfloat16)
 
-    for peer in peers:
-        pltpu.make_async_remote_copy(
-            src_ref=grad_hbm,
-            dst_ref=gathered.at[peer],
-            send_sem=gather_send.at[peer],
-            recv_sem=gather_recv.at[peer],
-            device_id={"slab": peer},
-            device_id_type=MESH,
-        ).wait_recv()
-
     mixed = [jnp.zeros((y_count, CHANNELS), jnp.float32) for _ in range(x_rows)]
-    for slot in range(n):
+    for slot in [me] + peers[::-1]:
+        if slot is not me:
+            pltpu.make_async_remote_copy(
+                src_ref=gathered.at[me],
+                dst_ref=gathered.at[slot],
+                send_sem=gather_send.at[slot],
+                recv_sem=gather_recv.at[slot],
+                device_id={"slab": slot},
+                device_id_type=MESH,
+            ).wait_recv()
         block = gathered[slot].astype(jnp.float32)
-        wide[pl.ds(slot * x_rows * y_count, x_rows * y_count), :] = block
+        rows = x_rows * y_count
+        wide[pl.ds(pl.multiple_of(slot * rows, 8), rows), :] = block
         for r in range(x_rows):
-            i = slot * x_rows + r
             row = block[r * y_count : (r + 1) * y_count, :]
+            factor = spread[pl.ds(slot * x_rows + r, 1), :]
             for x in range(x_rows):
-                mixed[x] += row * spread[i : i + 1, x * CHANNELS : (x + 1) * CHANNELS]
+                mixed[x] += row * factor[:, x * CHANNELS : (x + 1) * CHANNELS]
     grad_columns = jnp.concatenate(
         [
             wide[pl.ds(me * y_rows + y, x_count, stride=y_count), :]
@@ -310,7 +315,7 @@
             outgoing[slot, start : start + count, :] = term[slot * count : (slot + 1) * count]
             start += count
     terms = []
-    for peer in reversed(peers):
+    for peer in peers:
         copy = pltpu.make_async_remote_copy(
             src_ref=outgoing.at[peer],
             dst_ref=incoming.at[me],
@@ -329,7 +334,7 @@
         )
 
     total = outgoing[me]
-    for peer in peers:
+    for peer in peers[::-1]:
         pltpu.make_async_remote_copy(
             src_ref=outgoing.at[peer],
             dst_ref=incoming.at[peer],
@@ -411,8 +416,8 @@
     grad_values, factors = pl.pallas_call(
         functools.partial(gather_kernel, n, x_rows, y_rows),
         out_shape=(
-            jax.ShapeDtypeStruct(values.shape, values.dtype),
-            jax.ShapeDtypeStruct((term_rows, CHANNELS), jnp.float32),
+            pltpu.VMEM(values.shape, values.dtype),
+            pltpu.VMEM((term_rows, CHANNELS), jnp.float32),
         ),
         in_specs=[pl.BlockSpec(memory_space=pltpu.HBM)] * 7,
         out_specs=(vmem, vmem),
@@ -424,6 +429,7 @@
             pltpu.VMEM(key_x.shape, key_x.dtype),
             pltpu.VMEM(query_y.shape, query_y.dtype),
             pltpu.VMEM(key_y.shape, key_y.dtype),
+            pltpu.VMEM((x_count, x_rows * CHANNELS), jnp.float32),
             pltpu.VMEM((x_count * y_count, CHANNELS), jnp.float32),
             pltpu.VMEM((n, term_rows, CHANNELS), jnp.float32),
             pltpu.VMEM((n, term_rows, CHANNELS), jnp.float32),
@@ -433,15 +439,22 @@
             pltpu.SemaphoreType.DMA((n,)),
             pltpu.SemaphoreType.DMA((n,)),
         ],
-        compiler_params=pltpu.CompilerParams(collective_id=0, has_side_effects=True),
+        compiler_params=pltpu.CompilerParams(
+            collective_id=0, has_side_effects=True, vmem_limit_bytes=KERNEL_BYTES
+        ),
     )(
-        grad_out.reshape(x_rows * y_count, CHANNELS),
-        cached.transpose(1, 0, 2).reshape(y_rows * x_count, CHANNELS),
-        values.reshape(x_rows * y_count, CHANNELS),
-        query_x,
-        key_x,
-        query_y,
-        key_y,
+        *(
+            pltpu.with_memory_space_constraint(array, pltpu.HBM)
+            for array in (
+                grad_out.reshape(x_rows * y_count, CHANNELS),
+                cached.transpose(1, 0, 2).reshape(y_rows * x_count, CHANNELS),
+                values.reshape(x_rows * y_count, CHANNELS),
+                query_x,
+                key_x,
+                query_y,
+                key_y,
+            )
+        )
     )
     counts = (x_rows, x_rows, y_rows, y_rows)
     return pl.pallas_call(
@@ -450,10 +463,12 @@
         + tuple(jax.ShapeDtypeStruct((count, CHANNELS), jnp.float32) for count in counts),
         in_specs=[vmem] * 2,
         out_specs=(vmem,) * 5,
+        compiler_params=pltpu.CompilerParams(vmem_limit_bytes=KERNEL_BYTES),
     )(grad_values, factors)
 
 
 GATHERED_BYTES = 1 << 20
+KERNEL_BYTES = 16 << 20
 
 
 def on_device(n, *arrays):

time: 16.7 us -> 15.4 us (0.922)
  Pallas kernels: 15.8 us -> 14.5 us
    pallas_call x1, Pallas kernels: 1.33 us -> 0.62 us  [gathered_form(): pl.pallas_call(hand_out_kernel, out_shape=(jax.ShapeDtypeStruct(values.sh...]
    pallas_call x1, Pallas kernels: 14.4 us -> 13.9 us  [gathered_form(): pl.pallas_call(functools.partial(gather_kernel, n, x_rows, y_rows), out_s...]
where the time goes in v3:
time: 15.4 us; the launch traced here: 15.2 us
  Pallas kernels  14.5 us (94%)
  between operations  0.64 us (4%)
    pallas_call x1, Pallas kernels, gathered_form(): pl.pallas_call(functools.partial(gather_kernel, n, x_rows, y_rows), out_s...  13.9 us
    pallas_call x1, Pallas kernels, gathered_form(): pl.pallas_call(hand_out_kernel, out_shape=(jax.ShapeDtypeStruct(values.sh...  0.62 us

profile of v3, /device:TPU:0, one launch (start us, length us, event | category | flops | bytes accessed | tf_op | source)
XLA Modules:
  0.0 15.2 jit_solution(4561697919941251283)
XLA Ops:
  0.6 13.9 %shard_map.110 = (bf16[2,24,128]{2,1,0:T(8,128)(2,1)S(1)}, f32[10,128]{1,0:T(8,128)S(1)}) custom-call(bf16[48,128]{1,0:T(8,128)(2,1)} %bitcast.5, bf16[48,128]{1,0:T(8,128)(2,1)} %bitcast.6, bf16[48,128]{1,0:T(8,128)(2,1)} %bitcast.7, bf16[16,128]{1,0:T(8,128)(2,1)} %query_x_hbm.1, bf16[16,128]{1,0:T(8,128)(2,1)} %key_x_hbm.1, bf16[24,128]{1,0:T(8,128)(2,1)} %query_y_hbm.1, ...), custom_call_target="tpu_custom_call" | custom-call | tf_op jit(solution)/shard_map/pallas_call | solution.py:416
  14.6 0.6 %shard_map.111 = (bf16[2,24,128]{2,1,0:T(8,128)(2,1)}, f32[2,128]{1,0:T(2,128)}, f32[2,128]{1,0:T(2,128)}, f32[3,128]{1,0:T(4,128)}, f32[3,128]{1,0:T(4,128)}) custom-call(bf16[2,24,128]{2,1,0:T(8,128)(2,1)S(1)} %get-tuple-element.7.values_ref, f32[10,128]{1,0:T(8,128)S(1)} %get-tuple-element.8.factors_ref), custom_call_target="tpu_custom_call" | custom-call | tf_op jit(solution)/shard_map/pallas_call | solution.py:460

commit v4 on v3

--- a/solution.py
+++ b/solution.py
@@ -208,6 +208,10 @@
     peers = [
         lax.rem(me + step, n) for step in sorted(range(1, n), key=lambda s: abs(2 * s - n))
     ]
+    mate = me + 1 - 2 * lax.rem(me, 2)
+    far = [
+        lax.rem(me + step, n) for step in sorted(range(2, n, 2), key=lambda s: abs(2 * s - n))
+    ]
     x_count, y_count = query_x_ref.shape[0], query_y_ref.shape[0]
 
     own_grad = pltpu.make_async_copy(grad_hbm, gathered.at[me], own_sems.at[6])
@@ -231,18 +235,19 @@
         copy.start()
     own_grad.wait()
     pl.semaphore_wait(barrier, n - 1)
-    gathers = []
-    for peer in peers:
-        copy = pltpu.make_async_remote_copy(
-            src_ref=gathered.at[me],
-            dst_ref=gathered.at[me],
-            send_sem=gather_send.at[peer],
-            recv_sem=gather_recv.at[me],
-            device_id={"slab": peer},
+    def block_copy(block, target):
+        return pltpu.make_async_remote_copy(
+            src_ref=gathered.at[block],
+            dst_ref=gathered.at[block],
+            send_sem=gather_send.at[target, block],
+            recv_sem=gather_recv.at[block],
+            device_id={"slab": target},
             device_id_type=MESH,
         )
+
+    gathers = [block_copy(me, target) for target in far + [mate]]
+    for copy in gathers:
         copy.start()
-        gathers.append(copy)
 
     for copy in own:
         copy.wait()
@@ -271,16 +276,14 @@
     ).astype(jnp.bfloat16)
 
     mixed = [jnp.zeros((y_count, CHANNELS), jnp.float32) for _ in range(x_rows)]
-    for slot in [me] + peers[::-1]:
+    handed = [lax.rem(mate + step, n) for step in range(2, n, 2)]
+    for slot in [me, mate] + far[::-1] + handed:
         if slot is not me:
-            pltpu.make_async_remote_copy(
-                src_ref=gathered.at[me],
-                dst_ref=gathered.at[slot],
-                send_sem=gather_send.at[slot],
-                recv_sem=gather_recv.at[slot],
-                device_id={"slab": slot},
-                device_id_type=MESH,
-            ).wait_recv()
+            block_copy(slot, mate).wait_recv()
+        if any(slot is other for other in far):
+            copy = block_copy(slot, mate)
+            copy.start()
+            gathers.append(copy)
         block = gathered[slot].astype(jnp.float32)
         rows = x_rows * y_count
         wide[pl.ds(pl.multiple_of(slot * rows, 8), rows), :] = block
@@ -434,7 +437,7 @@
             pltpu.VMEM((n, term_rows, CHANNELS), jnp.float32),
             pltpu.VMEM((n, term_rows, CHANNELS), jnp.float32),
             pltpu.SemaphoreType.DMA((7,)),
-            pltpu.SemaphoreType.DMA((n,)),
+            pltpu.SemaphoreType.DMA((n, n)),
             pltpu.SemaphoreType.DMA((n,)),
             pltpu.SemaphoreType.DMA((n,)),
             pltpu.SemaphoreType.DMA((n,)),
@@ -472,7 +475,7 @@
 
 
 def on_device(n, *arrays):
-    if n > 1 and arrays[0].size * arrays[0].dtype.itemsize * n <= GATHERED_BYTES:
+    if n % 2 == 0 and arrays[0].size * arrays[0].dtype.itemsize * n <= GATHERED_BYTES:
         return gathered_form(n, *arrays)
     return exchanged_form(*arrays)
 

time: 15.4 us -> 16.1 us (1.045)
  Pallas kernels: 14.5 us -> 15.2 us
    pallas_call x1, Pallas kernels: 13.9 us -> 14.6 us  [gathered_form(): pl.pallas_call(functools.partial(gather_kernel, n, x_rows, y_rows), out_s...]
where the time goes in v4:
time: 16.1 us; the launch traced here: 15.8 us
  Pallas kernels  15.2 us (94%)
  between operations  0.64 us (4%)
    pallas_call x1, Pallas kernels, gathered_form(): pl.pallas_call(functools.partial(gather_kernel, n, x_rows, y_rows), out_s...  14.6 us
    pallas_call x1, Pallas kernels, gathered_form(): pl.pallas_call(hand_out_kernel, out_shape=(jax.ShapeDtypeStruct(values.sh...  0.62 us

profile of v4, /device:TPU:0, one launch (start us, length us, event | category | flops | bytes accessed | tf_op | source)
XLA Modules:
  0.0 15.8 jit_solution(1923181959400524948)
XLA Ops:
  0.6 14.6 %shard_map.110 = (bf16[2,24,128]{2,1,0:T(8,128)(2,1)S(1)}, f32[10,128]{1,0:T(8,128)S(1)}) custom-call(bf16[48,128]{1,0:T(8,128)(2,1)} %bitcast.5, bf16[48,128]{1,0:T(8,128)(2,1)} %bitcast.6, bf16[48,128]{1,0:T(8,128)(2,1)} %bitcast.7, bf16[16,128]{1,0:T(8,128)(2,1)} %query_x_hbm.1, bf16[16,128]{1,0:T(8,128)(2,1)} %key_x_hbm.1, bf16[24,128]{1,0:T(8,128)(2,1)} %query_y_hbm.1, ...), custom_call_target="tpu_custom_call" | custom-call | tf_op jit(solution)/shard_map/pallas_call | solution.py:419
  15.2 0.6 %shard_map.111 = (bf16[2,24,128]{2,1,0:T(8,128)(2,1)}, f32[2,128]{1,0:T(2,128)}, f32[2,128]{1,0:T(2,128)}, f32[3,128]{1,0:T(4,128)}, f32[3,128]{1,0:T(4,128)}) custom-call(bf16[2,24,128]{2,1,0:T(8,128)(2,1)S(1)} %get-tuple-element.7.values_ref, f32[10,128]{1,0:T(8,128)S(1)} %get-tuple-element.8.factors_ref), custom_call_target="tpu_custom_call" | custom-call | tf_op jit(solution)/shard_map/pallas_call | solution.py:463

commit v5 on v3

--- a/solution.py
+++ b/solution.py
@@ -194,6 +194,14 @@
     key_x_ref,
     query_y_ref,
     key_y_ref,
+    query_x,
+    query_y,
+    kernel_x,
+    kernel_x_turned,
+    kernel_y,
+    kernel_y_turned,
+    cached_lanes,
+    values_lanes,
     spread,
     wide,
     outgoing,
@@ -205,9 +213,8 @@
     term_recv,
 ):
     me = lax.axis_index("slab")
-    peers = [
-        lax.rem(me + step, n) for step in sorted(range(1, n), key=lambda s: abs(2 * s - n))
-    ]
+    late = me // (n // 2)
+    peers = [lax.rem(me + (2 * late - 1) * step + n, n) for step in range(1, n)]
     x_count, y_count = query_x_ref.shape[0], query_y_ref.shape[0]
 
     own_grad = pltpu.make_async_copy(grad_hbm, gathered.at[me], own_sems.at[6])
@@ -229,6 +236,37 @@
     ]
     for copy in own:
         copy.start()
+
+    def prepare():
+        for copy in own:
+            copy.wait()
+        for queries_ref, keys_ref, heads, kernel, turned in (
+            (query_x_ref, key_x_ref, query_x, kernel_x, kernel_x_turned),
+            (query_y_ref, key_y_ref, query_y, kernel_y, kernel_y_turned),
+        ):
+            heads[...] = by_head(queries_ref[...].astype(jnp.float32))
+            kernel[...], turned[...] = both_kernels(heads[...], keys_ref[...])
+        width = x_rows * CHANNELS
+        rows = lax.broadcasted_iota(jnp.int32, (x_count, width), 0)
+        lanes = lax.broadcasted_iota(jnp.int32, (x_count, width), 1)
+        own_columns = (rows == me * x_rows + lanes // CHANNELS).astype(jnp.bfloat16)
+        spread[...] = per_head(
+            jnp.dot(
+                kernel_x[...].astype(jnp.bfloat16),
+                own_columns,
+                preferred_element_type=jnp.float32,
+            )
+        )
+        for source, count, target in (
+            (cached_ref, x_count, cached_lanes),
+            (values_ref, y_count, values_lanes),
+        ):
+            array = source[...].astype(jnp.float32)
+            target[...] = jnp.concatenate(
+                [array[r : r + count] for r in range(0, array.shape[0], count)], axis=1
+            ).astype(jnp.bfloat16)
+
+    pl.when(late == 0)(prepare)
     own_grad.wait()
     pl.semaphore_wait(barrier, n - 1)
     gathers = []
@@ -243,32 +281,7 @@
         )
         copy.start()
         gathers.append(copy)
-
-    for copy in own:
-        copy.wait()
-    key_x, key_y = key_x_ref[...], key_y_ref[...]
-    query_x = by_head(query_x_ref[...].astype(jnp.float32))
-    query_y = by_head(query_y_ref[...].astype(jnp.float32))
-    kernel_x, kernel_x_turned = both_kernels(query_x, key_x)
-    kernel_y, kernel_y_turned = both_kernels(query_y, key_y)
-    width = x_rows * CHANNELS
-    rows = lax.broadcasted_iota(jnp.int32, (x_count, width), 0)
-    lanes = lax.broadcasted_iota(jnp.int32, (x_count, width), 1)
-    own_columns = (rows == me * x_rows + lanes // CHANNELS).astype(jnp.bfloat16)
-    spread[...] = per_head(
-        jnp.dot(
-            kernel_x.astype(jnp.bfloat16), own_columns, preferred_element_type=jnp.float32
-        )
-    )
-    kernel_y_low = kernel_y_turned.astype(jnp.bfloat16)
-    cached = cached_ref[...].astype(jnp.float32)
-    cached = jnp.concatenate(
-        [cached[y * x_count : (y + 1) * x_count] for y in range(y_rows)], axis=1
-    ).astype(jnp.bfloat16)
-    values = values_ref[...].astype(jnp.float32)
-    values = jnp.concatenate(
-        [values[x * y_count : (x + 1) * y_count] for x in range(x_rows)], axis=1
-    ).astype(jnp.bfloat16)
+    pl.when(late == 1)(prepare)
 
     mixed = [jnp.zeros((y_count, CHANNELS), jnp.float32) for _ in range(x_rows)]
     for slot in [me] + peers[::-1]:
@@ -299,10 +312,20 @@
     grad_columns = by_head(grad_columns)
     mixed = by_head(jnp.concatenate(mixed, axis=1).astype(jnp.bfloat16).astype(jnp.float32))
     query_x_term, key_x_term = factor_terms(
-        kernel_x, kernel_x_turned, grad_columns, cached, query_x, key_x
+        kernel_x[...],
+        kernel_x_turned[...],
+        grad_columns,
+        cached_lanes[...],
+        query_x[...],
+        key_x_ref[...],
     )
     query_y_term, key_y_term = factor_terms(
-        kernel_y, kernel_y_turned, mixed, values, query_y, key_y
+        kernel_y[...],
+        kernel_y_turned[...],
+        mixed,
+        values_lanes[...],
+        query_y[...],
+        key_y_ref[...],
     )
     for slot in range(n):
         start = 0
@@ -327,7 +350,9 @@
         copy.start()
         terms.append(copy)
 
-    grad_values = jnp.dot(kernel_y_low, mixed, preferred_element_type=jnp.float32)
+    grad_values = jnp.dot(
+        kernel_y_turned[...].astype(jnp.bfloat16), mixed, preferred_element_type=jnp.float32
+    )
     for x in range(x_rows):
         grad_values_ref[x] = grad_values[:, x * CHANNELS : (x + 1) * CHANNELS].astype(
             grad_values_ref.dtype
@@ -349,19 +374,25 @@
         copy.wait_send()
 
 
+def in_head(head, columns):
+    lanes = lax.broadcasted_iota(jnp.int32, (1, CHANNELS), 1)
+    mask = (lanes >= head * HEAD) & (lanes < (head + 1) * HEAD)
+    return jnp.concatenate([mask] * (columns // CHANNELS), axis=1)
+
+
 def by_head(array):
-    lanes = lax.broadcasted_iota(jnp.int32, array.shape, 1) % CHANNELS // HEAD
     return jnp.concatenate(
-        [jnp.where(lanes == head, array, 0.0) for head in range(HEADS)], axis=0
+        [jnp.where(in_head(head, array.shape[1]), array, 0.0) for head in range(HEADS)], axis=0
     ).astype(jnp.bfloat16)
 
 
 def per_head(array):
     rows = array.shape[0] // HEADS
-    lanes = lax.broadcasted_iota(jnp.int32, (rows, array.shape[1]), 1) % CHANNELS // HEAD
     picked = array[:rows]
     for head in range(1, HEADS):
-        picked = jnp.where(lanes == head, array[head * rows : (head + 1) * rows], picked)
+        picked = jnp.where(
+            in_head(head, array.shape[1]), array[head * rows : (head + 1) * rows], picked
+        )
     return picked
 
 
@@ -429,6 +460,14 @@
             pltpu.VMEM(key_x.shape, key_x.dtype),
             pltpu.VMEM(query_y.shape, query_y.dtype),
             pltpu.VMEM(key_y.shape, key_y.dtype),
+            pltpu.VMEM((HEADS * x_count, CHANNELS), jnp.bfloat16),
+            pltpu.VMEM((HEADS * y_count, CHANNELS), jnp.bfloat16),
+            pltpu.VMEM((HEADS * x_count, x_count), jnp.float32),
+            pltpu.VMEM((x_count, HEADS * x_count), jnp.float32),
+            pltpu.VMEM((HEADS * y_count, y_count), jnp.float32),
+            pltpu.VMEM((y_count, HEADS * y_count), jnp.float32),
+            pltpu.VMEM((x_count, y_rows * CHANNELS), jnp.bfloat16),
+            pltpu.VMEM((y_count, x_rows * CHANNELS), jnp.bfloat16),
             pltpu.VMEM((x_count, x_rows * CHANNELS), jnp.float32),
             pltpu.VMEM((x_count * y_count, CHANNELS), jnp.float32),
             pltpu.VMEM((n, term_rows, CHANNELS), jnp.float32),
@@ -472,7 +511,7 @@
 
 
 def on_device(n, *arrays):
-    if n > 1 and arrays[0].size * arrays[0].dtype.itemsize * n <= GATHERED_BYTES:
+    if n % 2 == 0 and arrays[0].size * arrays[0].dtype.itemsize * n <= GATHERED_BYTES:
         return gathered_form(n, *arrays)
     return exchanged_form(*arrays)
 

time: 15.4 us -> 14.8 us (0.961)
  Pallas kernels: 14.5 us -> 14 us
    pallas_call x1, Pallas kernels: 13.9 us -> 13.3 us  [gathered_form(): pl.pallas_call(functools.partial(gather_kernel, n, x_rows, y_rows), out_s...]
where the time goes in v5:
time: 14.8 us; the launch traced here: 14.6 us
  Pallas kernels  14 us (95%)
  between operations  0.64 us (4%)
    pallas_call x1, Pallas kernels, gathered_form(): pl.pallas_call(functools.partial(gather_kernel, n, x_rows, y_rows), out_s...  13.3 us
    pallas_call x1, Pallas kernels, gathered_form(): pl.pallas_call(hand_out_kernel, out_shape=(jax.ShapeDtypeStruct(values.sh...  0.62 us

profile of v5, /device:TPU:0, one launch (start us, length us, event | category | flops | bytes accessed | tf_op | source)
XLA Modules:
  0.0 14.6 jit_solution(10746184931700348672)
XLA Ops:
  0.6 13.3 %shard_map.110 = (bf16[2,24,128]{2,1,0:T(8,128)(2,1)S(1)}, f32[10,128]{1,0:T(8,128)S(1)}) custom-call(bf16[48,128]{1,0:T(8,128)(2,1)} %bitcast.5, bf16[48,128]{1,0:T(8,128)(2,1)} %bitcast.6, bf16[48,128]{1,0:T(8,128)(2,1)} %bitcast.7, bf16[16,128]{1,0:T(8,128)(2,1)} %query_x_hbm.1, bf16[16,128]{1,0:T(8,128)(2,1)} %key_x_hbm.1, bf16[24,128]{1,0:T(8,128)(2,1)} %query_y_hbm.1, ...), custom_call_target="tpu_custom_call" | custom-call | tf_op jit(solution)/shard_map/pallas_call | solution.py:447
  14.0 0.6 %shard_map.111 = (bf16[2,24,128]{2,1,0:T(8,128)(2,1)}, f32[2,128]{1,0:T(2,128)}, f32[2,128]{1,0:T(2,128)}, f32[3,128]{1,0:T(4,128)}, f32[3,128]{1,0:T(4,128)}) custom-call(bf16[2,24,128]{2,1,0:T(8,128)(2,1)S(1)} %get-tuple-element.7.values_ref, f32[10,128]{1,0:T(8,128)S(1)} %get-tuple-element.8.factors_ref), custom_call_target="tpu_custom_call" | custom-call | tf_op jit(solution)/shard_map/pallas_call | solution.py:499

commit v6 on v5

--- a/solution.py
+++ b/solution.py
@@ -204,6 +204,7 @@
     values_lanes,
     spread,
     wide,
+    packing,
     outgoing,
     incoming,
     own_sems,
@@ -216,6 +217,7 @@
     late = me // (n // 2)
     peers = [lax.rem(me + (2 * late - 1) * step + n, n) for step in range(1, n)]
     x_count, y_count = query_x_ref.shape[0], query_y_ref.shape[0]
+    term_rows = factors_ref.shape[0]
 
     own_grad = pltpu.make_async_copy(grad_hbm, gathered.at[me], own_sems.at[6])
     own_grad.start()
@@ -266,22 +268,34 @@
                 [array[r : r + count] for r in range(0, array.shape[0], count)], axis=1
             ).astype(jnp.bfloat16)
 
-    pl.when(late == 0)(prepare)
-    own_grad.wait()
-    pl.semaphore_wait(barrier, n - 1)
-    gathers = []
-    for peer in peers:
-        copy = pltpu.make_async_remote_copy(
-            src_ref=gathered.at[me],
-            dst_ref=gathered.at[me],
-            send_sem=gather_send.at[peer],
-            recv_sem=gather_recv.at[me],
-            device_id={"slab": peer},
-            device_id_type=MESH,
-        )
-        copy.start()
-        gathers.append(copy)
-    pl.when(late == 1)(prepare)
+    def gathers(source):
+        return [
+            pltpu.make_async_remote_copy(
+                src_ref=source,
+                dst_ref=gathered.at[me],
+                send_sem=gather_send.at[peer],
+                recv_sem=gather_recv.at[me],
+                device_id={"slab": peer},
+                device_id_type=MESH,
+            )
+            for peer in peers
+        ]
+
+    @pl.when(late == 0)
+    def _():
+        prepare()
+        own_grad.wait()
+        pl.semaphore_wait(barrier, n - 1)
+        for copy in gathers(gathered.at[me]):
+            copy.start()
+
+    @pl.when(late == 1)
+    def _():
+        pl.semaphore_wait(barrier, n - 1)
+        for copy in gathers(grad_hbm):
+            copy.start()
+        prepare()
+        own_grad.wait()
 
     mixed = [jnp.zeros((y_count, CHANNELS), jnp.float32) for _ in range(x_rows)]
     for slot in [me] + peers[::-1]:
@@ -327,20 +341,26 @@
         query_y[...],
         key_y_ref[...],
     )
-    for slot in range(n):
-        start = 0
-        for term, count in (
-            (query_x_term, x_rows),
-            (key_x_term, x_rows),
-            (query_y_term, y_rows),
-            (key_y_term, y_rows),
-        ):
-            outgoing[slot, start : start + count, :] = term[slot * count : (slot + 1) * count]
-            start += count
+    first = 0
+    for term, count in (
+        (query_x_term, x_rows),
+        (key_x_term, x_rows),
+        (query_y_term, y_rows),
+        (key_y_term, y_rows),
+    ):
+        packing[pl.ds(n * first, n * count), :] = term
+        for r in range(count):
+            outgoing[pl.ds(first + r, n, stride=term_rows), :] = packing[
+                pl.ds(n * first + r, n, stride=count), :
+            ]
+        first += count
+    def message(peer):
+        return pl.ds(pl.multiple_of(peer * term_rows, 8), term_rows)
+
     terms = []
     for peer in peers:
         copy = pltpu.make_async_remote_copy(
-            src_ref=outgoing.at[peer],
+            src_ref=outgoing.at[message(peer)],
             dst_ref=incoming.at[me],
             send_sem=term_send.at[peer],
             recv_sem=term_recv.at[me],
@@ -358,10 +378,12 @@
             grad_values_ref.dtype
         )
 
-    total = outgoing[me]
+    for copy in gathers(gathered.at[me]) + terms:
+        copy.wait_send()
+    total = outgoing[message(me), :]
     for peer in peers[::-1]:
         pltpu.make_async_remote_copy(
-            src_ref=outgoing.at[peer],
+            src_ref=outgoing.at[message(peer)],
             dst_ref=incoming.at[peer],
             send_sem=term_send.at[peer],
             recv_sem=term_recv.at[peer],
@@ -370,8 +392,6 @@
         ).wait_recv()
         total += incoming[peer]
     factors_ref[...] = total * (1.0 / math.sqrt(HEAD))
-    for copy in gathers + terms:
-        copy.wait_send()
 
 
 def in_head(head, columns):
@@ -442,7 +462,7 @@
 def gathered_form(n, grad_out, cached, values, query_x, key_x, query_y, key_y):
     x_rows, y_count = grad_out.shape[:2]
     x_count, y_rows = cached.shape[:2]
-    term_rows = 2 * (x_rows + y_rows)
+    term_rows = -(-2 * (x_rows + y_rows) // 8) * 8
     vmem = pl.BlockSpec(memory_space=pltpu.VMEM)
     grad_values, factors = pl.pallas_call(
         functools.partial(gather_kernel, n, x_rows, y_rows),
@@ -469,8 +489,9 @@
             pltpu.VMEM((x_count, y_rows * CHANNELS), jnp.bfloat16),
             pltpu.VMEM((y_count, x_rows * CHANNELS), jnp.bfloat16),
             pltpu.VMEM((x_count, x_rows * CHANNELS), jnp.float32),
-            pltpu.VMEM((x_count * y_count, CHANNELS), jnp.float32),
-            pltpu.VMEM((n, term_rows, CHANNELS), jnp.float32),
+            pltpu.VMEM(((x_count + 1) * y_count, CHANNELS), jnp.float32),
+            pltpu.VMEM((2 * (x_count + y_count) + 8, CHANNELS), jnp.float32),
+            pltpu.VMEM(((n + 1) * term_rows, CHANNELS), jnp.float32),
             pltpu.VMEM((n, term_rows, CHANNELS), jnp.float32),
             pltpu.SemaphoreType.DMA((7,)),
             pltpu.SemaphoreType.DMA((n,)),

time: 14.8 us -> 14.8 us (level)
  no operation moved by 1% of the time
where the time goes in v6:
time: 14.8 us; the launch traced here: 14.6 us
  Pallas kernels  14 us (95%)
  between operations  0.64 us (4%)
    pallas_call x1, Pallas kernels, gathered_form(): pl.pallas_call(functools.partial(gather_kernel, n, x_rows, y_rows), out_s...  13.4 us
    pallas_call x1, Pallas kernels, gathered_form(): pl.pallas_call(hand_out_kernel, out_shape=(jax.ShapeDtypeStruct(values.sh...  0.62 us

profile of v6, /device:TPU:0, one launch (start us, length us, event | category | flops | bytes accessed | tf_op | source)
XLA Modules:
  0.0 14.6 jit_solution(4506647694508886528)
XLA Ops:
  0.6 13.4 %shard_map.110 = (bf16[2,24,128]{2,1,0:T(8,128)(2,1)S(1)}, f32[16,128]{1,0:T(8,128)S(1)}) custom-call(bf16[48,128]{1,0:T(8,128)(2,1)} %bitcast.5, bf16[48,128]{1,0:T(8,128)(2,1)} %bitcast.6, bf16[48,128]{1,0:T(8,128)(2,1)} %bitcast.7, bf16[16,128]{1,0:T(8,128)(2,1)} %query_x_hbm.1, bf16[16,128]{1,0:T(8,128)(2,1)} %key_x_hbm.1, bf16[24,128]{1,0:T(8,128)(2,1)} %query_y_hbm.1, ...), custom_call_target="tpu_custom_call" | custom-call | tf_op jit(solution)/shard_map/pallas_call | solution.py:467
  14.0 0.6 %shard_map.111 = (bf16[2,24,128]{2,1,0:T(8,128)(2,1)}, f32[2,128]{1,0:T(2,128)}, f32[2,128]{1,0:T(2,128)}, f32[3,128]{1,0:T(4,128)}, f32[3,128]{1,0:T(4,128)}) custom-call(bf16[2,24,128]{2,1,0:T(8,128)(2,1)S(1)} %get-tuple-element.7.values_ref, f32[16,128]{1,0:T(8,128)S(1)} %get-tuple-element.8.factors_ref), custom_call_target="tpu_custom_call" | custom-call | tf_op jit(solution)/shard_map/pallas_call | solution.py:520

commit v7 on v6

--- a/solution.py
+++ b/solution.py
@@ -216,8 +216,10 @@
     me = lax.axis_index("slab")
     late = me // (n // 2)
     peers = [lax.rem(me + (2 * late - 1) * step + n, n) for step in range(1, n)]
+    mate = me + 1 - 2 * lax.rem(me, 2)
+    far = [lax.rem(me + (2 * late - 1) * step + n, n) for step in range(2, n, 2)]
+    handed = [lax.rem(mate + step, n) for step in range(2, n, 2)]
     x_count, y_count = query_x_ref.shape[0], query_y_ref.shape[0]
-    term_rows = factors_ref.shape[0]
 
     own_grad = pltpu.make_async_copy(grad_hbm, gathered.at[me], own_sems.at[6])
     own_grad.start()
@@ -268,18 +270,18 @@
                 [array[r : r + count] for r in range(0, array.shape[0], count)], axis=1
             ).astype(jnp.bfloat16)
 
+    def block_copy(source, block, target):
+        return pltpu.make_async_remote_copy(
+            src_ref=source,
+            dst_ref=gathered.at[block],
+            send_sem=gather_send.at[target, block],
+            recv_sem=gather_recv.at[block],
+            device_id={"slab": target},
+            device_id_type=MESH,
+        )
+
     def gathers(source):
-        return [
-            pltpu.make_async_remote_copy(
-                src_ref=source,
-                dst_ref=gathered.at[me],
-                send_sem=gather_send.at[peer],
-                recv_sem=gather_recv.at[me],
-                device_id={"slab": peer},
-                device_id_type=MESH,
-            )
-            for peer in peers
-        ]
+        return [block_copy(source, me, target) for target in far + [mate]]
 
     @pl.when(late == 0)
     def _():
@@ -298,16 +300,13 @@
         own_grad.wait()
 
     mixed = [jnp.zeros((y_count, CHANNELS), jnp.float32) for _ in range(x_rows)]
-    for slot in [me] + peers[::-1]:
+    hand_on = [block_copy(gathered.at[block], block, mate) for block in far]
+    for slot in [me, mate] + far + handed:
         if slot is not me:
-            pltpu.make_async_remote_copy(
-                src_ref=gathered.at[me],
-                dst_ref=gathered.at[slot],
-                send_sem=gather_send.at[slot],
-                recv_sem=gather_recv.at[slot],
-                device_id={"slab": slot},
-                device_id_type=MESH,
-            ).wait_recv()
+            block_copy(gathered.at[slot], slot, mate).wait_recv()
+        for block, copy in zip(far, hand_on):
+            if slot is block:
+                copy.start()
         block = gathered[slot].astype(jnp.float32)
         rows = x_rows * y_count
         wide[pl.ds(pl.multiple_of(slot * rows, 8), rows), :] = block
@@ -350,17 +349,14 @@
     ):
         packing[pl.ds(n * first, n * count), :] = term
         for r in range(count):
-            outgoing[pl.ds(first + r, n, stride=term_rows), :] = packing[
+            outgoing[:, first + r, :] = packing[
                 pl.ds(n * first + r, n, stride=count), :
             ]
         first += count
-    def message(peer):
-        return pl.ds(pl.multiple_of(peer * term_rows, 8), term_rows)
-
     terms = []
     for peer in peers:
         copy = pltpu.make_async_remote_copy(
-            src_ref=outgoing.at[message(peer)],
+            src_ref=outgoing.at[peer],
             dst_ref=incoming.at[me],
             send_sem=term_send.at[peer],
             recv_sem=term_recv.at[me],
@@ -378,12 +374,12 @@
             grad_values_ref.dtype
         )
 
-    for copy in gathers(gathered.at[me]) + terms:
+    for copy in gathers(gathered.at[me]) + hand_on + terms:
         copy.wait_send()
-    total = outgoing[message(me), :]
+    total = outgoing[me]
     for peer in peers[::-1]:
         pltpu.make_async_remote_copy(
-            src_ref=outgoing.at[message(peer)],
+            src_ref=outgoing.at[peer],
             dst_ref=incoming.at[peer],
             send_sem=term_send.at[peer],
             recv_sem=term_recv.at[peer],
@@ -462,7 +458,7 @@
 def gathered_form(n, grad_out, cached, values, query_x, key_x, query_y, key_y):
     x_rows, y_count = grad_out.shape[:2]
     x_count, y_rows = cached.shape[:2]
-    term_rows = -(-2 * (x_rows + y_rows) // 8) * 8
+    term_rows = 2 * (x_rows + y_rows)
     vmem = pl.BlockSpec(memory_space=pltpu.VMEM)
     grad_values, factors = pl.pallas_call(
         functools.partial(gather_kernel, n, x_rows, y_rows),
@@ -491,10 +487,10 @@
             pltpu.VMEM((x_count, x_rows * CHANNELS), jnp.float32),
             pltpu.VMEM(((x_count + 1) * y_count, CHANNELS), jnp.float32),
             pltpu.VMEM((2 * (x_count + y_count) + 8, CHANNELS), jnp.float32),
-            pltpu.VMEM(((n + 1) * term_rows, CHANNELS), jnp.float32),
+            pltpu.VMEM((n, term_rows, CHANNELS), jnp.float32),
             pltpu.VMEM((n, term_rows, CHANNELS), jnp.float32),
             pltpu.SemaphoreType.DMA((7,)),
-            pltpu.SemaphoreType.DMA((n,)),
+            pltpu.SemaphoreType.DMA((n, n)),
             pltpu.SemaphoreType.DMA((n,)),
             pltpu.SemaphoreType.DMA((n,)),
             pltpu.SemaphoreType.DMA((n,)),

time: 14.8 us -> 15.5 us (1.047)
  Pallas kernels: 14 us -> 14.6 us
    pallas_call x1, Pallas kernels: 13.4 us -> 14 us  [gathered_form(): pl.pallas_call(functools.partial(gather_kernel, n, x_rows, y_rows), out_s...]
where the time goes in v7:
time: 15.5 us; the launch traced here: 15.3 us
  Pallas kernels  14.6 us (94%)
  between operations  0.64 us (4%)
    pallas_call x1, Pallas kernels, gathered_form(): pl.pallas_call(functools.partial(gather_kernel, n, x_rows, y_rows), out_s...  14 us
    pallas_call x1, Pallas kernels, gathered_form(): pl.pallas_call(hand_out_kernel, out_shape=(jax.ShapeDtypeStruct(values.sh...  0.62 us

profile of v7, /device:TPU:0, one launch (start us, length us, event | category | flops | bytes accessed | tf_op | source)
XLA Modules:
  0.0 15.3 jit_solution(13150271026898579784)
XLA Ops:
  0.6 14.0 %shard_map.110 = (bf16[2,24,128]{2,1,0:T(8,128)(2,1)S(1)}, f32[10,128]{1,0:T(8,128)S(1)}) custom-call(bf16[48,128]{1,0:T(8,128)(2,1)} %bitcast.5, bf16[48,128]{1,0:T(8,128)(2,1)} %bitcast.6, bf16[48,128]{1,0:T(8,128)(2,1)} %bitcast.7, bf16[16,128]{1,0:T(8,128)(2,1)} %query_x_hbm.1, bf16[16,128]{1,0:T(8,128)(2,1)} %key_x_hbm.1, bf16[24,128]{1,0:T(8,128)(2,1)} %query_y_hbm.1, ...), custom_call_target="tpu_custom_call" | custom-call | tf_op jit(solution)/shard_map/pallas_call | solution.py:463
  14.7 0.6 %shard_map.111 = (bf16[2,24,128]{2,1,0:T(8,128)(2,1)}, f32[2,128]{1,0:T(2,128)}, f32[2,128]{1,0:T(2,128)}, f32[3,128]{1,0:T(4,128)}, f32[3,128]{1,0:T(4,128)}) custom-call(bf16[2,24,128]{2,1,0:T(8,128)(2,1)S(1)} %get-tuple-element.7.values_ref, f32[10,128]{1,0:T(8,128)S(1)} %get-tuple-element.8.factors_ref), custom_call_target="tpu_custom_call" | custom-call | tf_op jit(solution)/shard_map/pallas_call | solution.py:516

commit v8 on v6

--- a/solution.py
+++ b/solution.py
@@ -217,7 +217,6 @@
     late = me // (n // 2)
     peers = [lax.rem(me + (2 * late - 1) * step + n, n) for step in range(1, n)]
     x_count, y_count = query_x_ref.shape[0], query_y_ref.shape[0]
-    term_rows = factors_ref.shape[0]
 
     own_grad = pltpu.make_async_copy(grad_hbm, gathered.at[me], own_sems.at[6])
     own_grad.start()
@@ -350,17 +349,14 @@
     ):
         packing[pl.ds(n * first, n * count), :] = term
         for r in range(count):
-            outgoing[pl.ds(first + r, n, stride=term_rows), :] = packing[
+            outgoing[:, first + r, :] = packing[
                 pl.ds(n * first + r, n, stride=count), :
             ]
         first += count
-    def message(peer):
-        return pl.ds(pl.multiple_of(peer * term_rows, 8), term_rows)
-
     terms = []
     for peer in peers:
         copy = pltpu.make_async_remote_copy(
-            src_ref=outgoing.at[message(peer)],
+            src_ref=outgoing.at[peer],
             dst_ref=incoming.at[me],
             send_sem=term_send.at[peer],
             recv_sem=term_recv.at[me],
@@ -380,10 +376,10 @@
 
     for copy in gathers(gathered.at[me]) + terms:
         copy.wait_send()
-    total = outgoing[message(me), :]
+    total = outgoing[me]
     for peer in peers[::-1]:
         pltpu.make_async_remote_copy(
-            src_ref=outgoing.at[message(peer)],
+            src_ref=outgoing.at[peer],
             dst_ref=incoming.at[peer],
             send_sem=term_send.at[peer],
             recv_sem=term_recv.at[peer],
@@ -421,15 +417,10 @@
 
 
 def both_kernels(queries, key_rows):
-    kernels = []
-    for scores, axis in (
-        (rows_by_rows(queries, key_rows), 1),
-        (rows_by_rows(key_rows, queries), 0),
-    ):
-        scores = scores / math.sqrt(HEAD)
-        weights = jnp.exp(scores - jnp.max(scores, axis=axis, keepdims=True))
-        kernels.append(weights / jnp.sum(weights, axis=axis, keepdims=True))
-    return kernels
+    scores = rows_by_rows(key_rows, queries) / math.sqrt(HEAD)
+    weights = jnp.exp(scores - jnp.max(scores, axis=0, keepdims=True))
+    turned = weights / jnp.sum(weights, axis=0, keepdims=True)
+    return turned.T, turned
 
 
 def weighted_parts(kernel, coupling, axis):
@@ -462,7 +453,7 @@
 def gathered_form(n, grad_out, cached, values, query_x, key_x, query_y, key_y):
     x_rows, y_count = grad_out.shape[:2]
     x_count, y_rows = cached.shape[:2]
-    term_rows = -(-2 * (x_rows + y_rows) // 8) * 8
+    term_rows = 2 * (x_rows + y_rows)
     vmem = pl.BlockSpec(memory_space=pltpu.VMEM)
     grad_values, factors = pl.pallas_call(
         functools.partial(gather_kernel, n, x_rows, y_rows),
@@ -491,7 +482,7 @@
             pltpu.VMEM((x_count, x_rows * CHANNELS), jnp.float32),
             pltpu.VMEM(((x_count + 1) * y_count, CHANNELS), jnp.float32),
             pltpu.VMEM((2 * (x_count + y_count) + 8, CHANNELS), jnp.float32),
-            pltpu.VMEM(((n + 1) * term_rows, CHANNELS), jnp.float32),
+            pltpu.VMEM((n, term_rows, CHANNELS), jnp.float32),
             pltpu.VMEM((n, term_rows, CHANNELS), jnp.float32),
             pltpu.SemaphoreType.DMA((7,)),
             pltpu.SemaphoreType.DMA((n,)),

time: 14.8 us -> 14.8 us (level)
  no operation moved by 1% of the time
where the time goes in v8:
time: 14.8 us; the launch traced here: 14.6 us
  Pallas kernels  13.9 us (94%)
  between operations  0.64 us (4%)
    pallas_call x1, Pallas kernels, gathered_form(): pl.pallas_call(functools.partial(gather_kernel, n, x_rows, y_rows), out_s...  13.3 us
    pallas_call x1, Pallas kernels, gathered_form(): pl.pallas_call(hand_out_kernel, out_shape=(jax.ShapeDtypeStruct(values.sh...  0.62 us

profile of v8, /device:TPU:0, one launch (start us, length us, event | category | flops | bytes accessed | tf_op | source)
XLA Modules:
  0.0 14.6 jit_solution(14434008678251571092)
XLA Ops:
  0.6 13.3 %shard_map.110 = (bf16[2,24,128]{2,1,0:T(8,128)(2,1)S(1)}, f32[10,128]{1,0:T(8,128)S(1)}) custom-call(bf16[48,128]{1,0:T(8,128)(2,1)} %bitcast.5, bf16[48,128]{1,0:T(8,128)(2,1)} %bitcast.6, bf16[48,128]{1,0:T(8,128)(2,1)} %bitcast.7, bf16[16,128]{1,0:T(8,128)(2,1)} %query_x_hbm.1, bf16[16,128]{1,0:T(8,128)(2,1)} %key_x_hbm.1, bf16[24,128]{1,0:T(8,128)(2,1)} %query_y_hbm.1, ...), custom_call_target="tpu_custom_call" | custom-call | tf_op jit(solution)/shard_map/pallas_call | solution.py:458
  14.0 0.6 %shard_map.111 = (bf16[2,24,128]{2,1,0:T(8,128)(2,1)}, f32[2,128]{1,0:T(2,128)}, f32[2,128]{1,0:T(2,128)}, f32[3,128]{1,0:T(4,128)}, f32[3,128]{1,0:T(4,128)}) custom-call(bf16[2,24,128]{2,1,0:T(8,128)(2,1)S(1)} %get-tuple-element.7.values_ref, f32[10,128]{1,0:T(8,128)S(1)} %get-tuple-element.8.factors_ref), custom_call_target="tpu_custom_call" | custom-call | tf_op jit(solution)/shard_map/pallas_call | solution.py:511

commit v9 on v8

--- a/solution.py
+++ b/solution.py
@@ -267,10 +267,10 @@
                 [array[r : r + count] for r in range(0, array.shape[0], count)], axis=1
             ).astype(jnp.bfloat16)
 
-    def gathers(source):
+    def gathers():
         return [
             pltpu.make_async_remote_copy(
-                src_ref=source,
+                src_ref=gathered.at[me],
                 dst_ref=gathered.at[me],
                 send_sem=gather_send.at[peer],
                 recv_sem=gather_recv.at[me],
@@ -285,16 +285,16 @@
         prepare()
         own_grad.wait()
         pl.semaphore_wait(barrier, n - 1)
-        for copy in gathers(gathered.at[me]):
+        for copy in gathers():
             copy.start()
 
     @pl.when(late == 1)
     def _():
+        own_grad.wait()
         pl.semaphore_wait(barrier, n - 1)
-        for copy in gathers(grad_hbm):
+        for copy in gathers():
             copy.start()
         prepare()
-        own_grad.wait()
 
     mixed = [jnp.zeros((y_count, CHANNELS), jnp.float32) for _ in range(x_rows)]
     for slot in [me] + peers[::-1]:
@@ -374,7 +374,7 @@
             grad_values_ref.dtype
         )
 
-    for copy in gathers(gathered.at[me]) + terms:
+    for copy in gathers() + terms:
         copy.wait_send()
     total = outgoing[me]
     for peer in peers[::-1]:

time: 14.8 us -> 14.8 us (level)
  no operation moved by 1% of the time
where the time goes in v9:
time: 14.8 us; the launch traced here: 14.6 us
  Pallas kernels  13.9 us (94%)
  between operations  0.64 us (4%)
    pallas_call x1, Pallas kernels, gathered_form(): pl.pallas_call(functools.partial(gather_kernel, n, x_rows, y_rows), out_s...  13.3 us
    pallas_call x1, Pallas kernels, gathered_form(): pl.pallas_call(hand_out_kernel, out_shape=(jax.ShapeDtypeStruct(values.sh...  0.62 us

profile of v9, /device:TPU:0, one launch (start us, length us, event | category | flops | bytes accessed | tf_op | source)
XLA Modules:
  0.0 14.6 jit_solution(7589462506224408408)
XLA Ops:
  0.6 13.3 %shard_map.110 = (bf16[2,24,128]{2,1,0:T(8,128)(2,1)S(1)}, f32[10,128]{1,0:T(8,128)S(1)}) custom-call(bf16[48,128]{1,0:T(8,128)(2,1)} %bitcast.5, bf16[48,128]{1,0:T(8,128)(2,1)} %bitcast.6, bf16[48,128]{1,0:T(8,128)(2,1)} %bitcast.7, bf16[16,128]{1,0:T(8,128)(2,1)} %query_x_hbm.1, bf16[16,128]{1,0:T(8,128)(2,1)} %key_x_hbm.1, bf16[24,128]{1,0:T(8,128)(2,1)} %query_y_hbm.1, ...), custom_call_target="tpu_custom_call" | custom-call | tf_op jit(solution)/shard_map/pallas_call | solution.py:458
  14.0 0.6 %shard_map.111 = (bf16[2,24,128]{2,1,0:T(8,128)(2,1)}, f32[2,128]{1,0:T(2,128)}, f32[2,128]{1,0:T(2,128)}, f32[3,128]{1,0:T(4,128)}, f32[3,128]{1,0:T(4,128)}) custom-call(bf16[2,24,128]{2,1,0:T(8,128)(2,1)S(1)} %get-tuple-element.7.values_ref, f32[10,128]{1,0:T(8,128)S(1)} %get-tuple-element.8.factors_ref), custom_call_target="tpu_custom_call" | custom-call | tf_op jit(solution)/shard_map/pallas_call | solution.py:511
